TPU v7x, 512 devices: a whole 4x8x8 slice. The times are simulated.
512 devices in a mesh: ctx: 64 (over x, y_lo, z), width: 8 (over y_hi, core).
Axes of the slice: x: 4, y: 8 (y_hi: 4, y_lo: 2; y = y_hi * 2 + y_lo), z: 8, core: 2. Of those that a mesh axis runs over, the one named last changes fastest.
Arguments:
- queries: bfloat16 [512, 32768], P('width', 'ctx'), may hold values from -6 to 6
- keys: bfloat16 [512, 32768], P('width', 'ctx'), may hold values from -6 to 6
- values: bfloat16 [512, 32768], P('width', 'ctx'), may hold values from -6 to 6
- cotangent: bfloat16 [512, 32768], P('width', 'ctx'), may hold values from -6 to 6
- filters: float32 [32, 32768], P('width', 'ctx'), may hold values from -1.05 to 1.05
Outputs:
- mixed: bfloat16 [512, 32768], P('width', 'ctx')
- query_grad: bfloat16 [512, 32768], P('width', 'ctx')
- key_grad: bfloat16 [512, 32768], P('width', 'ctx')
- value_grad: bfloat16 [512, 32768], P('width', 'ctx')
- filter_grad: bfloat16 [32, 32768], P('width', 'ctx')
All inputs are finite; a program needn't handle non-finite values.
Results may differ from a plain program's by a relative error of at most 0.018.
Values may be sent and summed in bfloat16 or wider, within the bound.
No kernel may reach another device: no remote copies, remote signals or barrier semaphores. Data moves between devices by JAX's collectives and lax.ppermute only.
A program may use at most 64 MiB of HBM per device.

v0:
```python
import math

import jax
import jax.numpy as jnp
from jax import lax
from jax.sharding import PartitionSpec as P

GROUP = 16
FILTERS = 32
FIRST = 512


def angles(count_rows, count_cols, period, row_start):
    row_ids = row_start + jnp.arange(count_rows, dtype=jnp.int32)[:, None]
    col_ids = jnp.arange(count_cols, dtype=jnp.int32)[None, :]
    return (row_ids * col_ids % period).astype(jnp.float32) * (2.0 * math.pi / period)


def first_table(half_rows, period):
    grid = angles(half_rows, period, period, 0)
    cosine_part, sine_part = (jnp.cos(grid), jnp.sin(grid))
    return jnp.stack(
        [
            jnp.concatenate([cosine_part, -sine_part], 1),
            jnp.concatenate([sine_part, cosine_part], 1),
        ]
    ).astype(jnp.bfloat16)


def second_table(order_len):
    grid = angles(order_len, order_len, order_len, 0)
    cosine_part, sine_part = (jnp.cos(grid), jnp.sin(grid))
    return jnp.stack(
        [
            jnp.concatenate([cosine_part, -sine_part], 1),
            jnp.concatenate([sine_part, cosine_part], 1),
        ],
        axis=1,
    ).astype(jnp.bfloat16)


def back_table(order_len):
    grid = angles(order_len, order_len, order_len, 0)
    cosine_part, sine_part = (jnp.cos(grid), jnp.sin(grid))
    return jnp.concatenate(
        [
            jnp.concatenate([cosine_part, sine_part], 1),
            jnp.concatenate([-sine_part, cosine_part], 1),
        ],
        0,
    ).astype(jnp.bfloat16)


def last_table(period, half_rows):
    grid = angles(period, half_rows, period, 0)
    cosine_part, sine_part = (jnp.cos(grid), jnp.sin(grid))
    return jnp.stack(
        [jnp.stack([cosine_part, sine_part], 1), jnp.stack([-sine_part, cosine_part], 1)], 1
    ).astype(jnp.bfloat16)


def turn_forward(mixed, angle_grid):
    col_count = angle_grid.shape[1]
    real_part, imag_part = (mixed[..., :col_count], mixed[..., col_count:])
    cosine_part, sine_part = (jnp.cos(angle_grid), jnp.sin(angle_grid))
    return jnp.stack(
        [
            real_part * cosine_part + imag_part * sine_part,
            imag_part * cosine_part - real_part * sine_part,
        ],
        axis=-2,
    ).astype(jnp.bfloat16)


def turn_back(opened, angle_grid):
    col_count = angle_grid.shape[1]
    real_part, imag_part = (opened[..., :col_count], opened[..., col_count:])
    cosine_part, sine_part = (jnp.cos(angle_grid), jnp.sin(angle_grid))
    return jnp.stack(
        [
            real_part * cosine_part - imag_part * sine_part,
            imag_part * cosine_part + real_part * sine_part,
        ],
        axis=-2,
    ).astype(jnp.bfloat16)


def halves(spectrum):
    wide = spectrum.astype(jnp.float32)
    return (wide[..., :FIRST], wide[..., FIRST:])


def section_one(piece, table, angle_grid):
    mixed = jnp.einsum("srba,rbo->sao", piece, table, preferred_element_type=jnp.float32)
    return turn_forward(mixed, angle_grid)


def section_two(piece, table):
    return jnp.einsum("sprk,prq->skq", piece, table, preferred_element_type=jnp.float32).astype(
        jnp.bfloat16
    )


def section_back(spectrum, table, angle_grid):
    opened = jnp.einsum("skx,xo->sko", spectrum, table, preferred_element_type=jnp.float32)
    return turn_back(opened, angle_grid)


def section_last(piece, table, scale_out):
    row_blocks = jnp.einsum("sqra,qrxh->sxha", piece, table, preferred_element_type=jnp.float32)
    return (row_blocks * scale_out).astype(jnp.bfloat16)


def forward_both(complex_sig, real_sig, tables, twist_fwd):
    count = complex_sig.shape[0]
    complex_rows = complex_sig.reshape(count, 2, -1, FIRST)
    real_rows = real_sig.reshape(real_sig.shape[0], 1, -1, FIRST)
    joined = jnp.concatenate(
        [complex_rows, jnp.concatenate([real_rows, jnp.zeros_like(real_rows)], 1)], 0
    )

    def first_step(piece):
        return section_one(piece, tables[0], twist_fwd)

    turned = first_step(lax.all_to_all(joined, "ctx", split_axis=3, concat_axis=2, tiled=True))

    def second_step(piece):
        return section_two(piece, tables[1])

    spectra = second_step(lax.all_to_all(turned, "ctx", split_axis=3, concat_axis=1, tiled=True))
    return (spectra[:count], spectra[count:])


def forward_one(complex_sig, tables, twist_fwd):
    complex_rows = complex_sig.reshape(complex_sig.shape[0], 2, -1, FIRST)

    def first_step(piece):
        return section_one(piece, tables[0], twist_fwd)

    turned = first_step(
        lax.all_to_all(complex_rows, "ctx", split_axis=3, concat_axis=2, tiled=True)
    )

    def second_step(piece):
        return section_two(piece, tables[1])

    return second_step(lax.all_to_all(turned, "ctx", split_axis=3, concat_axis=1, tiled=True))


def inverse_both(complex_spec, real_spec, tables, twist_back, plain_scale):
    count = complex_spec.shape[0]
    joined = jnp.concatenate([complex_spec, real_spec], 0)

    def last_step(piece):
        return section_last(piece, tables[3], plain_scale)

    opened = last_step(
        lax.all_to_all(
            section_back(joined, tables[2], twist_back),
            "ctx",
            split_axis=3,
            concat_axis=1,
            tiled=True,
        )
    )
    arrived = lax.all_to_all(opened, "ctx", split_axis=2, concat_axis=3, tiled=True)
    arrived = arrived.reshape(arrived.shape[0], 2, -1)
    return (arrived[:count], arrived[count:])


def inverse_one(complex_spec, tables, twist_back, plain_scale):

    def last_step(piece):
        return section_last(piece, tables[3], plain_scale)

    opened = last_step(
        lax.all_to_all(
            section_back(complex_spec, tables[2], twist_back),
            "ctx",
            split_axis=3,
            concat_axis=1,
            tiled=True,
        )
    )
    arrived = lax.all_to_all(opened, "ctx", split_axis=2, concat_axis=3, tiled=True)
    return arrived.reshape(arrived.shape[0], 2, -1)


def on_device(queries, keys, values, cotangent, filters):
    chan_count, local_len = queries.shape
    ctx_size = lax.axis_size("ctx")
    ctx_pos = lax.axis_index("ctx")
    length = local_len * ctx_size
    full_span = 2 * length
    half_rows = length // FIRST
    second_len = 2 * half_rows
    part_a = FIRST // ctx_size
    part_k = second_len // ctx_size
    groups = chan_count // (2 * FILTERS)
    signal_count = groups * FILTERS
    tables = (
        first_table(half_rows, second_len),
        second_table(FIRST),
        back_table(FIRST),
        last_table(second_len, half_rows),
    )
    twist_fwd = angles(part_a, second_len, full_span, ctx_pos * part_a)
    twist_back = angles(part_k, FIRST, full_span, ctx_pos * part_k)
    plain_scale = 1.0 / full_span
    root_scale = 1.0 / math.sqrt(GROUP * length)

    def pack(array):
        return (
            array.reshape(groups, 2, FILTERS, local_len)
            .transpose(0, 2, 1, 3)
            .reshape(signal_count, 2, local_len)
        )

    def unpack(array):
        return (
            array.reshape(groups, FILTERS, 2, local_len)
            .transpose(0, 2, 1, 3)
            .reshape(chan_count, local_len)
        )

    prod_sig = pack((keys.astype(jnp.float32) * values.astype(jnp.float32)).astype(jnp.bfloat16))
    grad_sig = pack(
        (cotangent.astype(jnp.float32) * queries.astype(jnp.float32)).astype(jnp.bfloat16)
    )
    taps = filters.astype(jnp.bfloat16)
    taps = lax.all_gather(taps, "width", axis=0, tiled=True)
    prod_spec, taps_spec = forward_both(prod_sig, taps, tables, twist_fwd)
    taps_real, taps_imag = halves(taps_spec.reshape(1, FILTERS, part_k, 2 * FIRST))
    prod_four = prod_spec.reshape(groups, FILTERS, part_k, 2 * FIRST)
    prod_real, prod_imag = halves(prod_four)
    resp_spec = jnp.concatenate(
        [
            taps_real * prod_real - taps_imag * prod_imag,
            taps_real * prod_imag + taps_imag * prod_real,
        ],
        -1,
    )
    resp_spec = resp_spec.astype(jnp.bfloat16).reshape(signal_count, part_k, 2 * FIRST)
    response = inverse_one(resp_spec, tables, twist_back, plain_scale)
    grad_spec = forward_one(grad_sig, tables, twist_fwd)
    grad_four = grad_spec.reshape(groups, FILTERS, part_k, 2 * FIRST)
    grad_real, grad_imag = halves(grad_four)
    pull_spec = jnp.concatenate(
        [
            taps_real * grad_real + taps_imag * grad_imag,
            taps_real * grad_imag - taps_imag * grad_real,
        ],
        -1,
    )
    pull_spec = pull_spec.astype(jnp.bfloat16).reshape(signal_count, part_k, 2 * FIRST)
    prod_part_real, prod_part_imag = halves(prod_four)
    grad_part_real, grad_part_imag = halves(grad_four)
    real_sum = jnp.sum(grad_part_real * prod_part_real + grad_part_imag * prod_part_imag, 0)
    imag_sum = jnp.sum(grad_part_imag * prod_part_real - grad_part_real * prod_part_imag, 0)
    lag_total = lax.psum_scatter(
        jnp.concatenate([real_sum, imag_sum], -1), "width", scatter_dimension=0, tiled=True
    )
    lag_spec = (lag_total * root_scale).astype(jnp.bfloat16)
    pulled, lag_sig = inverse_both(pull_spec, lag_spec, tables, twist_back, plain_scale)
    response_wide = unpack(response).astype(jnp.float32)
    pulled_wide = unpack(pulled).astype(jnp.float32)
    mixed = (queries.astype(jnp.float32) * response_wide).astype(jnp.bfloat16)
    query_grad = (cotangent.astype(jnp.float32) * response_wide).astype(jnp.bfloat16)
    key_grad = (pulled_wide * values.astype(jnp.float32)).astype(jnp.bfloat16)
    value_grad = (pulled_wide * keys.astype(jnp.float32)).astype(jnp.bfloat16)
    return (mixed, query_grad, key_grad, value_grad, lag_sig[:, 0, :])


def solution(mesh):
    in_specs = (
        P("width", "ctx"),
        P("width", "ctx"),
        P("width", "ctx"),
        P("width", "ctx"),
        P("width", "ctx"),
    )
    out_specs = (
        P("width", "ctx"),
        P("width", "ctx"),
        P("width", "ctx"),
        P("width", "ctx"),
        P("width", "ctx"),
    )
    return jax.shard_map(
        on_device, mesh=mesh, in_specs=in_specs, out_specs=out_specs, check_vma=False
    )
```

profile of v0, /device:TPU:6, one launch (start us, length us, event | category | flops | bytes accessed | tf_op | source)
XLA Modules:
  0.0 250.1 jit_solution(13246361345260870626)
XLA Ops:
  7.2 0.9 fusion.40
  9.3 15.0 %all-to-all-start.4 = ((bf16[64,2,256]{2,1,0:T(2,128)(2,1)}), bf16[64,2,256]{2,1,0:T(2,128)(2,1)S(1)}, u32[]{:S(2)}, u32[]{:S(2)}) async-start(bf16[64,2,256]{2,1,0:T(2,128)(2,1)} %reshape.312), calls=%async_computation.4 | async-start | bytes 131072 | tf_op jit(solution)/shard_map/all_to_all | solution.py:141
  24.3 4.3 %negate_convert_fusion = (bf16[512,512]{1,0:T(8,128)(2,1)S(1)}, bf16[512,512]{1,0:T(8,128)(2,1)S(1)}) fusion(), kind=kLoop, calls=%fused_computation.30 | loop fusion | flops 4456448 | bytes 1048576 | tf_op jit(solution)/shard_map/convert.42
  28.7 4.0 %fusion.27 = bf16[512,512]{1,0:T(8,128)(2,1)S(1)} fusion(), kind=kLoop, calls=%fused_computation.42 | loop fusion | flops 3932160 | bytes 524288 | tf_op jit(solution)/shard_map/convert.38
  33.9 16.0 %all-gather = bf16[8,4,512]{2,1,0:T(4,128)(2,1)S(1)} all-gather(bf16[1,4,512]{2,1,0:T(4,128)(2,1)S(1)} %convert_bitcast_fusion), channel_id=1, replica_groups=mesh['ctx'=64,'width'=8] {'width'}, dimensions={0}, use_global_device_ids=true | all-gather | bytes 36864 | tf_op jit(solution)/shard_map/all_gather | solution.py:231
  49.9 1.3 maximum_bitcast_fusion.18
  53.1 11.3 %all-to-all-start = ((bf16[64,2,512]{2,1,0:T(2,128)(2,1)}), bf16[64,2,512]{2,1,0:T(2,128)(2,1)S(1)}, u32[]{:S(2)}, u32[]{:S(2)}) async-start(bf16[64,2,512]{2,1,0:T(2,128)(2,1)} %reshape.304), calls=%async_computation | async-start | bytes 262144 | tf_op jit(solution)/shard_map/all_to_all | solution.py:125
  65.6 1.1 reshape.314
  66.7 6.9 %all-to-all-done = bf16[64,2,512]{2,1,0:T(2,128)(2,1)S(1)} async-done(((bf16[64,2,512]{2,1,0:T(2,128)(2,1)}), bf16[64,2,512]{2,1,0:T(2,128)(2,1)S(1)}, u32[]{:S(2)}, u32[]{:S(2)}) %all-to-all-start) | async-done | bytes 131104 | tf_op jit(solution)/shard_map/all_to_all | solution.py:125
  73.6 6.5 %all-to-all-start.5 = ((bf16[64,2,512]{2,1,0:T(2,128)(2,1)}), bf16[64,2,512]{2,1,0:T(2,128)(2,1)S(1)}, u32[]{:S(2)}, u32[]{:S(2)}) async-start(bf16[64,2,512]{2,1,0:T(2,128)(2,1)} %reshape.314), calls=%async_computation.5 | async-start | bytes 262144 | tf_op jit(solution)/shard_map/all_to_all | solution.py:147
  81.6 1.0 reshape.306
  82.6 6.0 %all-to-all-done.5 = bf16[64,2,512]{2,1,0:T(2,128)(2,1)S(1)} async-done(((bf16[64,2,512]{2,1,0:T(2,128)(2,1)}), bf16[64,2,512]{2,1,0:T(2,128)(2,1)S(1)}, u32[]{:S(2)}, u32[]{:S(2)}) %all-to-all-start.5) | async-done | bytes 131104 | tf_op jit(solution)/shard_map/all_to_all | solution.py:147
  88.6 6.8 %all-to-all-start.1 = ((bf16[64,2,1024]{2,1,0:T(2,128)(2,1)}), bf16[64,2,1024]{2,1,0:T(2,128)(2,1)S(1)}, u32[]{:S(2)}, u32[]{:S(2)}) async-start(bf16[64,2,1024]{2,1,0:T(2,128)(2,1)} %reshape.306), calls=%async_computation.1 | async-start | bytes 524288 | tf_op jit(solution)/shard_map/all_to_all | solution.py:130
  95.6 1.1 reshape.315
  96.7 1.9 fusion.14
  98.7 6.0 %all-to-all-done.1 = bf16[64,2,1024]{2,1,0:T(2,128)(2,1)S(1)} async-done(((bf16[64,2,1024]{2,1,0:T(2,128)(2,1)}), bf16[64,2,1024]{2,1,0:T(2,128)(2,1)S(1)}, u32[]{:S(2)}, u32[]{:S(2)}) %all-to-all-start.1) | async-done | bytes 262176 | tf_op jit(solution)/shard_map/all_to_all | solution.py:130
  104.6 1.2 reshape.307
  105.8 1.9 fusion.5
  108.8 1.1 reshape.308
  109.9 7.6 %all-to-all-start.2 = ((bf16[64,2,512]{2,1,0:T(2,128)(2,1)}), bf16[64,2,512]{2,1,0:T(2,128)(2,1)S(1)}, u32[]{:S(2)}, u32[]{:S(2)}) async-start(bf16[64,2,512]{2,1,0:T(2,128)(2,1)} %reshape.308), calls=%async_computation.2 | async-start | bytes 262144 | tf_op jit(solution)/shard_map/all_to_all | solution.py:177
  118.4 1.3 dynamic-slice
  120.3 5.7 %all-to-all-done.2 = bf16[64,2,512]{2,1,0:T(2,128)(2,1)S(1)} async-done(((bf16[64,2,512]{2,1,0:T(2,128)(2,1)}), bf16[64,2,512]{2,1,0:T(2,128)(2,1)S(1)}, u32[]{:S(2)}, u32[]{:S(2)}) %all-to-all-start.2) | async-done | bytes 131104 | tf_op jit(solution)/shard_map/all_to_all | solution.py:177
  128.2 6.9 %all-to-all-start.3 = ((bf16[64,2,256]{2,1,0:T(2,128)(2,1)}), bf16[64,2,256]{2,1,0:T(2,128)(2,1)S(1)}, u32[]{:S(2)}, u32[]{:S(2)}) async-start(bf16[64,2,256]{2,1,0:T(2,128)(2,1)} %reshape.310), calls=%async_computation.3 | async-start | bytes 131072 | tf_op jit(solution)/shard_map/all_to_all | solution.py:185
  135.1 63.0 %all-reduce.4.cloned.1.call-done = f32[32,2,1024]{2,0,1:T(8,128)} async-done(((f32[32,2,1024]{2,0,1:T(8,128)}), f32[32,2,1024]{2,0,1:T(8,128)}) %all-reduce.4.cloned.1.call-update) | async-done | bytes 262160
  198.1 0.9 fusion.66
  200.0 1.4 reshape.316
  201.4 11.1 %all-to-all-start.6 = ((bf16[64,2,576]{2,1,0:T(2,128)(2,1)}), bf16[64,2,576]{2,1,0:T(2,128)(2,1)S(1)}, u32[]{:S(2)}, u32[]{:S(2)}) async-start(bf16[64,2,576]{2,1,0:T(2,128)(2,1)} %reshape.316), calls=%async_computation.6 | async-start | bytes 327680 | tf_op jit(solution)/shard_map/all_to_all | solution.py:158
  213.5 7.7 %all-to-all-done.6 = bf16[64,2,576]{2,1,0:T(2,128)(2,1)S(1)} async-done(((bf16[64,2,576]{2,1,0:T(2,128)(2,1)}), bf16[64,2,576]{2,1,0:T(2,128)(2,1)S(1)}, u32[]{:S(2)}, u32[]{:S(2)}) %all-to-all-start.6) | async-done | bytes 147488 | tf_op jit(solution)/shard_map/all_to_all | solution.py:158
  223.1 1.0 reshape.318
  224.2 7.0 %all-to-all-start.7 = ((bf16[64,2,288]{2,1,0:T(2,128)(2,1)}), bf16[64,2,288]{2,1,0:T(2,128)(2,1)S(1)}, u32[]{:S(2)}, u32[]{:S(2)}) async-start(bf16[64,2,288]{2,1,0:T(2,128)(2,1)} %reshape.318), calls=%async_computation.7 | async-start | bytes 196608 | tf_op jit(solution)/shard_map/all_to_all | solution.py:166
  231.9 7.8 %all-to-all-done.7 = bf16[64,2,288]{2,1,0:T(2,128)(2,1)S(1)} async-done(((bf16[64,2,288]{2,1,0:T(2,128)(2,1)}), bf16[64,2,288]{2,1,0:T(2,128)(2,1)S(1)}, u32[]{:S(2)}, u32[]{:S(2)}) %all-to-all-start.7) | async-done | bytes 73760 | tf_op jit(solution)/shard_map/all_to_all | solution.py:166
  241.5 1.0 copy.153
  (107 shorter events, 18.1 us)
Async XLA Ops:
  8.4 25.4 %copy-start.16 = (f32[4,512]{1,0:T(4,128)S(1)}, f32[4,512]{1,0:T(4,128)}, u32[]{:S(2)}) copy-start(f32[4,512]{1,0:T(4,128)} %param.9) | copy-start | bytes 24580
  8.4 41.4 %copy-start.6 = (bf16[64,512]{1,0:T(8,128)(2,1)S(1)}, bf16[64,512]{1,0:T(8,128)(2,1)}, u32[]{:S(2)}) copy-start(bf16[64,512]{1,0:T(8,128)(2,1)} %param.7) | copy-start | bytes 196612
  8.4 41.4 %copy-start.8 = (bf16[64,512]{1,0:T(8,128)(2,1)S(1)}, bf16[64,512]{1,0:T(8,128)(2,1)}, u32[]{:S(2)}) copy-start(bf16[64,512]{1,0:T(8,128)(2,1)} %param.6) | copy-start | bytes 196612
  9.3 43.8 %all-to-all-start.4 = ((bf16[64,2,256]{2,1,0:T(2,128)(2,1)}), bf16[64,2,256]{2,1,0:T(2,128)(2,1)S(1)}, u32[]{:S(2)}, u32[]{:S(2)}) async-start(bf16[64,2,256]{2,1,0:T(2,128)(2,1)} %reshape.312), calls=%async_computation.4 | async-start | bytes 131072 | tf_op jit(solution)/shard_map/all_to_all | solution.py:141
  33.8 31.2 %copy-start.12 = (f32[8,128]{1,0:T(8,128)}, f32[8,128]{1,0:T(8,128)S(1)}, u32[]{:S(2)}) copy-start(f32[8,128]{1,0:T(8,128)S(1)} %get-tuple-element.35) | copy-start | bytes 12292
  33.9 31.2 %copy-start.14 = (f32[8,128]{1,0:T(8,128)}, f32[8,128]{1,0:T(8,128)S(1)}, u32[]{:S(2)}) copy-start(f32[8,128]{1,0:T(8,128)S(1)} %get-tuple-element.36) | copy-start | bytes 12292
  53.0 12.1 %copy-start = (bf16[1,64,256]{2,1,0:T(8,128)(2,1)}, bf16[1,64,256]{2,1,0:T(8,128)(2,1)S(1)}, u32[]{:S(2)}) copy-start(bf16[1,64,256]{2,1,0:T(8,128)(2,1)S(1)} %get-tuple-element.31) | copy-start | bytes 98308
  53.0 12.1 %copy-start.2 = (bf16[1,64,256]{2,1,0:T(8,128)(2,1)}, bf16[1,64,256]{2,1,0:T(8,128)(2,1)S(1)}, u32[]{:S(2)}) copy-start(bf16[1,64,256]{2,1,0:T(8,128)(2,1)S(1)} %get-tuple-element.32) | copy-start | bytes 98308
  53.1 20.5 %all-to-all-start = ((bf16[64,2,512]{2,1,0:T(2,128)(2,1)}), bf16[64,2,512]{2,1,0:T(2,128)(2,1)S(1)}, u32[]{:S(2)}, u32[]{:S(2)}) async-start(bf16[64,2,512]{2,1,0:T(2,128)(2,1)} %reshape.304), calls=%async_computation | async-start | bytes 262144 | tf_op jit(solution)/shard_map/all_to_all | solution.py:125
  65.6 15.1 %copy-start.1 = (bf16[1,64,256]{2,1,0:T(8,128)(2,1)S(1)}, bf16[1,64,256]{2,1,0:T(8,128)(2,1)}, u32[]{:S(2)}) copy-start(bf16[1,64,256]{2,1,0:T(8,128)(2,1)} %copy-done) | copy-start | bytes 98308
  65.6 15.1 %copy-start.3 = (bf16[1,64,256]{2,1,0:T(8,128)(2,1)S(1)}, bf16[1,64,256]{2,1,0:T(8,128)(2,1)}, u32[]{:S(2)}) copy-start(bf16[1,64,256]{2,1,0:T(8,128)(2,1)} %copy-done.2) | copy-start | bytes 98308
  66.7 14.3 %copy-start.13 = (f32[8,128]{1,0:T(8,128)S(1)}, f32[8,128]{1,0:T(8,128)}, u32[]{:S(2)}) copy-start(f32[8,128]{1,0:T(8,128)} %copy-done.12) | copy-start | bytes 12292
  66.7 14.3 %copy-start.15 = (f32[8,128]{1,0:T(8,128)S(1)}, f32[8,128]{1,0:T(8,128)}, u32[]{:S(2)}) copy-start(f32[8,128]{1,0:T(8,128)} %copy-done.14) | copy-start | bytes 12292
  73.6 15.0 %all-to-all-start.5 = ((bf16[64,2,512]{2,1,0:T(2,128)(2,1)}), bf16[64,2,512]{2,1,0:T(2,128)(2,1)S(1)}, u32[]{:S(2)}, u32[]{:S(2)}) async-start(bf16[64,2,512]{2,1,0:T(2,128)(2,1)} %reshape.314), calls=%async_computation.5 | async-start | bytes 262144 | tf_op jit(solution)/shard_map/all_to_all | solution.py:147
  88.6 16.0 %all-to-all-start.1 = ((bf16[64,2,1024]{2,1,0:T(2,128)(2,1)}), bf16[64,2,1024]{2,1,0:T(2,128)(2,1)S(1)}, u32[]{:S(2)}, u32[]{:S(2)}) async-start(bf16[64,2,1024]{2,1,0:T(2,128)(2,1)} %reshape.306), calls=%async_computation.1 | async-start | bytes 524288 | tf_op jit(solution)/shard_map/all_to_all | solution.py:130
  109.9 8.5 %copy-start.10 = (bf16[128,1,64]{0,2,1:T(8,128)(2,1)S(1)}, bf16[128,1,64]{0,2,1:T(8,128)(2,1)}, u32[]{:S(2)}) copy-start(bf16[128,1,64]{0,2,1:T(8,128)(2,1)} %get-tuple-element.42) | copy-start | bytes 49156
  109.9 8.5 %copy-start.11 = (bf16[128,1,64]{0,2,1:T(8,128)(2,1)S(1)}, bf16[128,1,64]{0,2,1:T(8,128)(2,1)}, u32[]{:S(2)}) copy-start(bf16[128,1,64]{0,2,1:T(8,128)(2,1)} %fusion.76) | copy-start | bytes 49156
  109.9 16.1 %all-to-all-start.2 = ((bf16[64,2,512]{2,1,0:T(2,128)(2,1)}), bf16[64,2,512]{2,1,0:T(2,128)(2,1)S(1)}, u32[]{:S(2)}, u32[]{:S(2)}) async-start(bf16[64,2,512]{2,1,0:T(2,128)(2,1)} %reshape.308), calls=%async_computation.2 | async-start | bytes 262144 | tf_op jit(solution)/shard_map/all_to_all | solution.py:177
  117.5 80.5 %all-reduce.4.cloned.1.call-start = ((), (), s32[]{:S(2)}) async-start(), calls=%async_computation.8 | async-start | bytes 524288
  128.2 73.2 %all-to-all-start.3 = ((bf16[64,2,256]{2,1,0:T(2,128)(2,1)}), bf16[64,2,256]{2,1,0:T(2,128)(2,1)S(1)}, u32[]{:S(2)}, u32[]{:S(2)}) async-start(bf16[64,2,256]{2,1,0:T(2,128)(2,1)} %reshape.310), calls=%async_computation.3 | async-start | bytes 131072 | tf_op jit(solution)/shard_map/all_to_all | solution.py:185
  201.4 19.8 %all-to-all-start.6 = ((bf16[64,2,576]{2,1,0:T(2,128)(2,1)}), bf16[64,2,576]{2,1,0:T(2,128)(2,1)S(1)}, u32[]{:S(2)}, u32[]{:S(2)}) async-start(bf16[64,2,576]{2,1,0:T(2,128)(2,1)} %reshape.316), calls=%async_computation.6 | async-start | bytes 327680 | tf_op jit(solution)/shard_map/all_to_all | solution.py:158
  222.1 9.1 %copy-start.4 = (bf16[64,512]{1,0:T(8,128)(2,1)S(1)}, bf16[64,512]{1,0:T(8,128)(2,1)}, u32[]{:S(2)}) copy-start(bf16[64,512]{1,0:T(8,128)(2,1)} %param.8) | copy-start | bytes 196612
  222.1 9.1 %copy-start.5 = (bf16[64,512]{1,0:T(8,128)(2,1)S(1)}, bf16[64,512]{1,0:T(8,128)(2,1)}, u32[]{:S(2)}) copy-start(bf16[64,512]{1,0:T(8,128)(2,1)} %param.5) | copy-start | bytes 196612
  224.2 15.4 %all-to-all-start.7 = ((bf16[64,2,288]{2,1,0:T(2,128)(2,1)}), bf16[64,2,288]{2,1,0:T(2,128)(2,1)S(1)}, u32[]{:S(2)}, u32[]{:S(2)}) async-start(bf16[64,2,288]{2,1,0:T(2,128)(2,1)} %reshape.318), calls=%async_computation.7 | async-start | bytes 196608 | tf_op jit(solution)/shard_map/all_to_all | solution.py:166
  239.9 0.9 copy-start.7
  239.9 0.9 copy-start.9
Sparse Core Ops, SparseCore 0:
  121.3 76.7 all-reduce.3
where the time goes:
time: 252 us; the launch traced here: 250 us
  waiting for transfers between devices  103 us (41%)
  starting transfers between devices  72.3 us (29%)
  local copies, waits for them, and re-layouts  21.7 us (9%)
  other arithmetic  16.1 us (6%)
  blocking collectives  16 us (6%)
  between operations  15.4 us (6%)
  matrix products  5.73 us (2%)
    unnamed x2, waiting for transfers between devices  63 us
    all_gather x1, blocking collectives, on_device(): taps = lax.all_gather(taps, 'width', axis=0, tiled=True)  16 us
    all_to_all x1, starting transfers between devices, forward_one(): lax.all_to_all(complex_rows, 'ctx', split_axis=3, concat_axis=2, tiled=True)  15 us
    unnamed x54, local copies, waits for them, and re-layouts  14.7 us
    all_to_all x1, starting transfers between devices, forward_both(): lax.all_to_all(joined, 'ctx', split_axis=3, concat_axis=2, tiled=True)  11.3 us
    all_to_all x1, starting transfers between devices, inverse_both(): lax.all_to_all(section_back(joined, tables[2], twist_back), 'ctx', split_...  11.1 us
    another operation x6, other arithmetic  10.1 us
    all_to_all x1, waiting for transfers between devices, inverse_both(): lax.all_to_all(opened, 'ctx', split_axis=2, concat_axis=3, tiled=True)  7.76 us
  transfers between devices with their start and end apart: 9, of which 7 were waited for; matrix products, arithmetic and copies ran while one was open for 12% of the time, Pallas kernels for 0%

commit v1 on v0

v1 whole, which is shorter than its diff:
```python
import functools
import math

import jax
import jax.numpy as jnp
import ml_dtypes
import numpy as np
from jax import lax
from jax.experimental import pallas as pl
from jax.experimental.pallas import tpu as pltpu
from jax.sharding import PartitionSpec as P

GROUP = 16
LENGTH = 32768
SPAN = 65536
LANES = 128
COLS = 512
ROWS = LENGTH // LANES
CTX = 64
SUB = 4
AXES = ("ctx", "width")


def grid_angles(rows, cols, period):
    grid = np.outer(np.arange(rows), np.arange(cols)) % period
    return grid * (2.0 * math.pi / period)


def tables():
    def low(array):
        return np.asarray(array, dtype=np.float32).astype(ml_dtypes.bfloat16)

    grid = grid_angles(COLS, ROWS, COLS)
    first = low(np.concatenate([np.cos(grid), -np.sin(grid)], 0))
    last = low(np.concatenate([np.cos(grid.T), -np.sin(grid.T)], 1))
    grid = grid_angles(LANES, LANES, LANES)
    cosine, sine = np.cos(grid), np.sin(grid)
    second = low(np.block([[cosine, -sine], [sine, cosine]]))
    back = low(np.block([[cosine, sine], [-sine, cosine]]))
    grid = grid_angles(COLS, LANES, SPAN)
    twist = np.concatenate([np.cos(grid), np.sin(grid)], 1).astype(np.float32)
    return first, second, back, last, twist


def dot(left, right):
    return jnp.dot(left, right, preferred_element_type=jnp.float32)


def low(array):
    return array.astype(jnp.bfloat16)


def wide(array):
    return array.astype(jnp.float32)


def rows_of(piece):
    pairs = piece.reshape(CTX // 2, 2, SUB, piece.shape[-1])
    joined = jnp.concatenate([pairs[:, 0], pairs[:, 1]], axis=1)
    return joined.reshape(CTX * SUB, piece.shape[-1])


def pieces_of(rows):
    return rows.reshape(rows.shape[0] // SUB, SUB, rows.shape[1])


def turn(real, imag, twist, sign):
    cosine, sine = twist[:, :LANES], twist[:, LANES:]
    if sign < 0:
        return real * cosine + imag * sine, imag * cosine - real * sine
    return real * cosine - imag * sine, imag * cosine + real * sine


def spectrum(opened, twist, second):
    real, imag = turn(opened[:COLS], opened[COLS:], twist, -1)
    return dot(low(jnp.concatenate([real, imag], 1)), second)


def unturned(real, imag, back, twist):
    opened = dot(low(jnp.concatenate([real, imag], 1)), back)
    return turn(opened[:, :LANES], opened[:, LANES:], twist, 1)


def pack_kernel(keys, values, cotangent, queries, filters, out, prods, grads, taps):
    width = lax.axis_index("width")
    prod = wide(keys[...]) * wide(values[...])
    grad = wide(cotangent[...]) * wide(queries[...])
    for s in range(SUB):
        lanes = slice(LANES * s, LANES * (s + 1))
        prods[pl.ds(s, CTX, stride=SUB), :] = prod[:, lanes]
        grads[pl.ds(s, CTX, stride=SUB), :] = grad[:, lanes]
        taps[pl.ds(s, SUB, stride=SUB), :] = filters[:, lanes]
    own = taps[...]
    for block in range(8):
        for half in range(2):
            rows = pl.ds(16 * block + 128 * half, 16)
            piece = jnp.concatenate([prods[rows, :], grads[rows, :], own], 1)
            place = 8 * jnp.bitwise_xor(width, block) + 4 * half
            out[pl.ds(place, 4)] = low(pieces_of(piece))


def spread_kernel(arrived, first, second, back, last, twist, prod_out, grad_out, lag_out):
    pair = rows_of(wide(arrived[:, :, : 2 * LANES]))
    opened = dot(first[...], low(pair))
    turns = twist[...]
    prod = spectrum(opened[:, :LANES], turns, second[...])
    grad = spectrum(opened[:, LANES:], turns, second[...])
    prod_out[...] = low(prod)
    grad_out[...] = low(grad)
    prod_real, prod_imag = prod[:, :LANES], prod[:, LANES:]
    grad_real, grad_imag = grad[:, :LANES], grad[:, LANES:]
    real, imag = unturned(
        grad_real * prod_real + grad_imag * prod_imag,
        grad_imag * prod_real - grad_real * prod_imag,
        back[...],
        turns,
    )
    lag = dot(last[...], low(jnp.concatenate([real, imag], 0)))
    lag = lag * (1.0 / (SPAN * math.sqrt(GROUP * LENGTH)))
    lag_out[...] = low(pieces_of(lag))


def filter_kernel(arrived, prod, grad, first, second, back, last, twist, out):
    turns = twist[...]
    opened = dot(first[...], low(rows_of(wide(arrived[...]))))
    taps = spectrum(opened, turns, second[...])
    taps_real, taps_imag = taps[:, :LANES], taps[:, LANES:]
    prod_real, prod_imag = wide(prod[:, :LANES]), wide(prod[:, LANES:])
    grad_real, grad_imag = wide(grad[:, :LANES]), wide(grad[:, LANES:])
    real = taps_real * (prod_real - grad_imag) - taps_imag * (prod_imag - grad_real)
    imag = taps_real * (prod_imag + grad_real) + taps_imag * (prod_real + grad_imag)
    real, imag = unturned(real, imag, back[...], turns)
    real, imag = low(real), low(imag)
    stacked = jnp.concatenate(
        [jnp.concatenate([real, imag], 1), jnp.concatenate([imag, -real], 1)], 0
    )
    both = dot(last[...], stacked) * (1.0 / SPAN)
    out[...] = low(pieces_of(both))


def gate_kernel(
    arrived, keys, values, cotangent, queries, mixed, query_grad, key_grad, value_grad, filter_grad, resps, pulls
):
    width = lax.axis_index("width")
    for block in range(8):
        for half in range(2):
            place = 8 * jnp.bitwise_xor(width, block) + 4 * half
            piece = wide(arrived[pl.ds(place, 4), :, : 2 * LANES]).reshape(16, 2 * LANES)
            rows = pl.ds(16 * block + 128 * half, 16)
            resps[rows, :] = piece[:, :LANES]
            pulls[rows, :] = piece[:, LANES:]
    lag = wide(arrived[:, :, 2 * LANES :]).reshape(GROUP, SUB, SUB, LANES)
    lag = jnp.sum(lag, 0)
    for s in range(SUB):
        lanes = slice(LANES * s, LANES * (s + 1))
        response = resps[pl.ds(s, CTX, stride=SUB), :]
        pulled = pulls[pl.ds(s, CTX, stride=SUB), :]
        mixed[:, lanes] = low(wide(queries[:, lanes]) * response)
        query_grad[:, lanes] = low(wide(cotangent[:, lanes]) * response)
        key_grad[:, lanes] = low(pulled * wide(values[:, lanes]))
        value_grad[:, lanes] = low(pulled * wide(keys[:, lanes]))
        filter_grad[:, lanes] = low(lag[:, s, :])


def shape(*dims):
    return jax.ShapeDtypeStruct(dims, jnp.bfloat16)


def call(kernel, out_shape, scratch=(), flops=0, **kwargs):
    return pl.pallas_call(
        kernel,
        out_shape=out_shape,
        scratch_shapes=scratch,
        cost_estimate=pl.CostEstimate(flops=flops, bytes_accessed=1 << 20, transcendentals=0),
        compiler_params=pltpu.CompilerParams(vmem_limit_bytes=24 << 20),
        **kwargs,
    )


def on_device(first, second, back, last, twist, queries, keys, values, cotangent, filters):
    pairs = [
        (c * 8 + w, c * 8 + (w ^ (c // 8))) for c in range(CTX) for w in range(8)
    ]
    channels, local = queries.shape
    packed = call(
        pack_kernel,
        shape(CTX, SUB, 3 * LANES),
        (
            pltpu.VMEM((channels * SUB, LANES), jnp.float32),
            pltpu.VMEM((channels * SUB, LANES), jnp.float32),
            pltpu.VMEM((SUB * SUB, LANES), jnp.float32),
        ),
    )(keys, values, cotangent, queries, filters)
    arrived = lax.all_to_all(packed, "ctx", split_axis=0, concat_axis=0, tiled=True)
    taps = lax.ppermute(arrived[:, :, 2 * LANES :], AXES, pairs)
    prod, grad, lag = call(
        spread_kernel,
        (shape(COLS, 2 * LANES), shape(COLS, 2 * LANES), shape(CTX, SUB, LANES)),
        flops=400_000_000,
    )(arrived, first, second, back, last, twist)
    lag = lax.ppermute(lag, AXES, pairs)
    both = call(
        filter_kernel, shape(CTX, SUB, 2 * LANES), flops=340_000_000
    )(taps, prod, grad, first, second, back, last, twist)
    outgoing = jnp.concatenate([both, lag], -1)
    returned = lax.all_to_all(outgoing, "ctx", split_axis=0, concat_axis=0, tiled=True)
    full = shape(channels, local)
    return call(
        gate_kernel,
        (full, full, full, full, shape(SUB, local)),
        (pltpu.VMEM((channels * SUB, LANES), jnp.float32),) * 2,
    )(returned, keys, values, cotangent, queries)


def solution(mesh):
    spec = P("width", "ctx")
    fixed = tables()
    mapped = jax.shard_map(
        on_device,
        mesh=mesh,
        in_specs=(P(),) * len(fixed) + (spec,) * 5,
        out_specs=(spec,) * 5,
        check_vma=False,
    )

    def run(queries, keys, values, cotangent, filters):
        return mapped(*fixed, queries, keys, values, cotangent, filters)

    return run
```

time: 252 us -> 69.6 us (0.28)
  the two profiles are of different devices: /device:TPU:6 before, /device:TPU:9 now
where the time goes in v1:
time: 69.6 us; the launch traced here: 69.1 us
  blocking collectives  53.4 us (77%)
  local copies, waits for them, and re-layouts  6.23 us (9%)
  starting transfers between devices  5.47 us (8%)
  Pallas kernels  2.86 us (4%)
  between operations  0.76 us (1%)
    all_to_all x1, blocking collectives, on_device(): lax.all_to_all(outgoing, 'ctx', split_axis=0, concat_axis=0, tiled=True)  27.9 us
    all_to_all x1, blocking collectives, on_device(): lax.all_to_all(packed, 'ctx', split_axis=0, concat_axis=0, tiled=True)  25.5 us
    unnamed x24, local copies, waits for them, and re-layouts  6.21 us
    ppermute x1, starting transfers between devices, on_device(): taps = lax.ppermute(arrived[:, :, 2 * LANES:], AXES, pairs)  3.55 us
    ppermute x1, starting transfers between devices, on_device(): lag = lax.ppermute(lag, AXES, pairs)  1.92 us
  transfers between devices with their start and end apart: 2, of which 1 were waited for; matrix products, arithmetic and copies ran while one was open for 0% of the time, Pallas kernels for 3%

profile of v1, /device:TPU:9, one launch (start us, length us, event | category | flops | bytes accessed | tf_op | source)
XLA Modules:
  0.0 69.1 jit_solution(17837507752097766464)
XLA Ops:
  0.6 0.0 copy-start
  0.6 0.0 copy-start.6
  0.7 0.9 %copy-done.6 = bf16[64,512]{1,0:T(8,128)(2,1)S(1)} copy-done((bf16[64,512]{1,0:T(8,128)(2,1)S(1)}, bf16[64,512]{1,0:T(8,128)(2,1)}, u32[]{:S(2)}) %copy-start.6) | copy-done | bytes 65560
  1.5 0.0 copy-start.7
  1.5 0.8 %copy-done.7 = bf16[64,512]{1,0:T(8,128)(2,1)S(1)} copy-done((bf16[64,512]{1,0:T(8,128)(2,1)S(1)}, bf16[64,512]{1,0:T(8,128)(2,1)}, u32[]{:S(2)}) %copy-start.7) | copy-done | bytes 65560
  2.4 0.0 copy-start.8
  2.4 0.8 %copy-done.8 = bf16[64,512]{1,0:T(8,128)(2,1)S(1)} copy-done((bf16[64,512]{1,0:T(8,128)(2,1)S(1)}, bf16[64,512]{1,0:T(8,128)(2,1)}, u32[]{:S(2)}) %copy-start.8) | copy-done | bytes 65560
  3.2 0.0 copy-start.9
  3.2 0.8 %copy-done.9 = bf16[64,512]{1,0:T(8,128)(2,1)S(1)} copy-done((bf16[64,512]{1,0:T(8,128)(2,1)S(1)}, bf16[64,512]{1,0:T(8,128)(2,1)}, u32[]{:S(2)}) %copy-start.9) | copy-done | bytes 65560
  4.1 0.0 copy-start.11
  4.1 0.7 %copy-done.11 = f32[4,512]{1,0:T(4,128)S(1)} copy-done((f32[4,512]{1,0:T(4,128)S(1)}, f32[4,512]{1,0:T(4,128)}, u32[]{:S(2)}) %copy-start.11) | copy-done | bytes 8216
  4.8 0.1 shard_map.137
  4.8 0.0 copy-start.5
  4.9 25.5 %all_to_all.10.arrived = bf16[64,4,384]{2,1,0:T(4,128)(2,1)S(1)} all-to-all(bf16[64,4,384]{2,1,0:T(4,128)(2,1)S(1)} %shard_map.137), channel_id=1, replica_groups=mesh['ctx'=64,'width'=8] {'ctx'}, dimensions={0} | all-to-all | bytes 393216 | tf_op jit(solution)/shard_map/all_to_all | solution.py:194
  30.4 3.5 %collective-permute-start = (bf16[64,4,128]{2,1,0:T(4,128)(2,1)S(1)}, bf16[64,4,128]{2,1,0:T(4,128)(2,1)S(1)}, u32[]{:S(2)}, u32[]{:S(2)}) collective-permute-start(bf16[64,4,128]{2,1,0:T(4,128)(2,1)S(1)} %slice.4), channel_id=1, source_target_pairs={{0,0},{1,1},{2,2},{3,3},{4,4},{5,5},{6,6},{7,7},{8,8},{9,9},{10,10... | collective-permute-start | bytes 196616 | tf_op jit(solution)/shard_map/ppermute | solution.py:195
  33.9 0.0 copy-done
  33.9 0.0 copy-done.5
  33.9 0.0 copy-done.4
  34.0 0.0 copy-start.1
  34.0 1.0 %copy-done.1 = bf16[256,1024]{1,0:T(8,128)(2,1)S(1)} copy-done((bf16[256,1024]{1,0:T(8,128)(2,1)S(1)}, bf16[256,1024]{1,0:T(8,128)(2,1)}, u32[]{:S(2)}) %copy-start.1) | copy-done | bytes 524312
  35.0 1.0 %copy-done.2 = bf16[1024,256]{1,0:T(8,128)(2,1)S(1)} copy-done((bf16[1024,256]{1,0:T(8,128)(2,1)S(1)}, bf16[1024,256]{1,0:T(8,128)(2,1)}, u32[]{:S(2)}) %copy-start.2) | copy-done | bytes 524312
  36.0 1.1 %shard_map.138 = (bf16[512,256]{1,0:T(8,128)(2,1)S(1)}, bf16[512,256]{1,0:T(8,128)(2,1)S(1)}, bf16[64,4,128]{2,1,0:T(4,128)(2,1)S(1)}) custom-call(bf16[64,4,384]{2,1,0:T(4,128)(2,1)S(1)} %all_to_all.10.arrived, bf16[1024,256]{1,0:T(8,128)(2,1)S(1)} %copy-done.2, bf16[256,256]{1,0:T(8,128)(2,1)S(1)} %copy-done.5, bf16[256,256]{1,0:T(8,128)(2,1)S(1)} %copy-done.4, ...), custom_call_target="tpu_custom_call" | custom-call | flops 400000000 | bytes 1048576 | tf_op jit(solution)/shard_map/pallas_call | solution.py:196
  37.1 1.9 %collective-permute-start.1 = (bf16[64,4,128]{2,1,0:T(4,128)(2,1)S(1)}, bf16[64,4,128]{2,1,0:T(4,128)(2,1)S(1)}, u32[]{:S(2)}, u32[]{:S(2)}) collective-permute-start(bf16[64,4,128]{2,1,0:T(4,128)(2,1)S(1)} %get-tuple-element.10), channel_id=1, source_target_pairs={{0,0},{1,1},{2,2},{3,3},{4,4},{5,5},{6,6},{7,7},{8,8},{9,9},{10,10... | collective-permute-start | bytes 196616 | tf_op jit(solution)/shard_map/ppermute | solution.py:201
  39.1 0.0 collective-permute-done.arrived
  39.1 0.0 copy-done.3
  39.1 0.9 %shard_map.139 = bf16[64,4,256]{2,1,0:T(4,128)(2,1)S(1)} custom-call(bf16[64,4,128]{2,1,0:T(4,128)(2,1)S(1)} %collective-permute-done.arrived, bf16[512,256]{1,0:T(8,128)(2,1)S(1)} %get-tuple-element.8.prod, bf16[512,256]{1,0:T(8,128)(2,1)S(1)} %get-tuple-element.9.grad, bf16[1024,256]{1,0:T(8,128)(2,1)S(1)} %copy-done.3, bf16[256,256]{1,0:T(8,128)(2,1)S(1)} %copy-done.5, ...), custom_call_target="tpu_custom_call" | custom-call | flops 340000000 | bytes 1048576 | tf_op jit(solution)/shard_map/pallas_call | solution.py:202
  40.0 0.3 collective-permute-done.1
  40.3 0.1 pad_maximum_fusion
  40.4 0.0 copy-start.10
  40.4 27.9 %all_to_all.11.arrived = bf16[64,4,384]{2,1,0:T(4,128)(2,1)S(1)} all-to-all(bf16[64,4,384]{2,1,0:T(4,128)(2,1)S(1)} %pad_maximum_fusion), channel_id=1, replica_groups=mesh['ctx'=64,'width'=8] {'ctx'}, dimensions={0} | all-to-all | bytes 393216 | tf_op jit(solution)/shard_map/all_to_all | solution.py:206
  68.3 0.0 copy-done.10
  68.3 0.8 %shard_map.140 = (bf16[64,512]{1,0:T(8,128)(2,1)}, bf16[64,512]{1,0:T(8,128)(2,1)}, bf16[64,512]{1,0:T(8,128)(2,1)}, bf16[64,512]{1,0:T(8,128)(2,1)}, bf16[4,512]{1,0:T(4,128)(2,1)}) custom-call(bf16[64,4,384]{2,1,0:T(4,128)(2,1)S(1)} %all_to_all.11.arrived, bf16[64,512]{1,0:T(8,128)(2,1)S(1)} %copy-done.6, bf16[64,512]{1,0:T(8,128)(2,1)S(1)} %copy-done.7, ...), custom_call_target="tpu_custom_call" | custom-call | bytes 1048576 | tf_op jit(solution)/shard_map/pallas_call | solution.py:208
  (4 shorter events, 0.0 us)
Async XLA Ops:
  0.6 33.3 %copy-start = (f32[512,256]{1,0:T(8,128)S(1)}, f32[512,256]{1,0:T(8,128)}, u32[]{:S(2)}) copy-start(f32[512,256]{1,0:T(8,128)} %constant.14.clone.twist) | copy-start | bytes 1572868
  0.6 0.9 %copy-start.6 = (bf16[64,512]{1,0:T(8,128)(2,1)S(1)}, bf16[64,512]{1,0:T(8,128)(2,1)}, u32[]{:S(2)}) copy-start(bf16[64,512]{1,0:T(8,128)(2,1)} %keys.3) | copy-start | bytes 196612
  1.5 0.8 %copy-start.7 = (bf16[64,512]{1,0:T(8,128)(2,1)S(1)}, bf16[64,512]{1,0:T(8,128)(2,1)}, u32[]{:S(2)}) copy-start(bf16[64,512]{1,0:T(8,128)(2,1)} %values.3) | copy-start | bytes 196612
  2.4 0.8 %copy-start.8 = (bf16[64,512]{1,0:T(8,128)(2,1)S(1)}, bf16[64,512]{1,0:T(8,128)(2,1)}, u32[]{:S(2)}) copy-start(bf16[64,512]{1,0:T(8,128)(2,1)} %cotangent.3) | copy-start | bytes 196612
  3.2 0.8 %copy-start.9 = (bf16[64,512]{1,0:T(8,128)(2,1)S(1)}, bf16[64,512]{1,0:T(8,128)(2,1)}, u32[]{:S(2)}) copy-start(bf16[64,512]{1,0:T(8,128)(2,1)} %queries.3) | copy-start | bytes 196612
  4.1 0.7 %copy-start.11 = (f32[4,512]{1,0:T(4,128)S(1)}, f32[4,512]{1,0:T(4,128)}, u32[]{:S(2)}) copy-start(f32[4,512]{1,0:T(4,128)} %filters.1) | copy-start | bytes 24580
  4.8 29.1 %copy-start.5 = (bf16[256,256]{1,0:T(8,128)(2,1)S(1)}, bf16[256,256]{1,0:T(8,128)(2,1)}, u32[]{:S(2)}) copy-start(bf16[256,256]{1,0:T(8,128)(2,1)} %constant.11.clone.second) | copy-start | bytes 393220
  30.3 3.6 %copy-start.4 = (bf16[256,256]{1,0:T(8,128)(2,1)S(1)}, bf16[256,256]{1,0:T(8,128)(2,1)}, u32[]{:S(2)}) copy-start(bf16[256,256]{1,0:T(8,128)(2,1)} %constant.12.clone.back) | copy-start | bytes 393220
  30.4 8.7 %collective-permute-start = (bf16[64,4,128]{2,1,0:T(4,128)(2,1)S(1)}, bf16[64,4,128]{2,1,0:T(4,128)(2,1)S(1)}, u32[]{:S(2)}, u32[]{:S(2)}) collective-permute-start(bf16[64,4,128]{2,1,0:T(4,128)(2,1)S(1)} %slice.4), channel_id=1, source_target_pairs={{0,0},{1,1},{2,2},{3,3},{4,4},{5,5},{6,6},{7,7},{8,8},{9,9},{10,10... | collective-permute-start | bytes 196616 | tf_op jit(solution)/shard_map/ppermute | solution.py:195
  34.0 1.0 %copy-start.1 = (bf16[256,1024]{1,0:T(8,128)(2,1)S(1)}, bf16[256,1024]{1,0:T(8,128)(2,1)}, u32[]{:S(2)}) copy-start(bf16[256,1024]{1,0:T(8,128)(2,1)} %constant.13.clone.last) | copy-start | bytes 1572868
  35.0 1.0 %copy-start.2 = (bf16[1024,256]{1,0:T(8,128)(2,1)S(1)}, bf16[1024,256]{1,0:T(8,128)(2,1)}, u32[]{:S(2)}) copy-start(bf16[1024,256]{1,0:T(8,128)(2,1)} %constant.10.clone.first) | copy-start | bytes 1572868
  36.0 3.0 %copy-start.3 = (bf16[1024,256]{1,0:T(8,128)(2,1)S(1)}, bf16[1024,256]{1,0:T(8,128)(2,1)}, u32[]{:S(2)}) copy-start(bf16[1024,256]{1,0:T(8,128)(2,1)} %constant.10.clone.first) | copy-start | bytes 1572868
  37.1 3.1 %collective-permute-start.1 = (bf16[64,4,128]{2,1,0:T(4,128)(2,1)S(1)}, bf16[64,4,128]{2,1,0:T(4,128)(2,1)S(1)}, u32[]{:S(2)}, u32[]{:S(2)}) collective-permute-start(bf16[64,4,128]{2,1,0:T(4,128)(2,1)S(1)} %get-tuple-element.10), channel_id=1, source_target_pairs={{0,0},{1,1},{2,2},{3,3},{4,4},{5,5},{6,6},{7,7},{8,8},{9,9},{10,10... | collective-permute-start | bytes 196616 | tf_op jit(solution)/shard_map/ppermute | solution.py:201
  40.4 27.9 %copy-start.10 = (bf16[64,512]{1,0:T(8,128)(2,1)S(1)}, bf16[64,512]{1,0:T(8,128)(2,1)}, u32[]{:S(2)}) copy-start(bf16[64,512]{1,0:T(8,128)(2,1)} %queries.3) | copy-start | bytes 196612

commit v2 on v1

--- a/solution.py
+++ b/solution.py
@@ -1,4 +1,3 @@
-import functools
 import math
 
 import jax
@@ -81,7 +80,45 @@
     return turn(opened[:, :LANES], opened[:, LANES:], twist, 1)
 
 
-def pack_kernel(keys, values, cotangent, queries, filters, out, prods, grads, taps):
+def stretch(width, block, half):
+    turn_by = jnp.bitwise_xor(width, block)
+    odd, high, core = (turn_by // 2) % 2, turn_by // 4, turn_by % 2
+    mixed = 1 - jnp.bitwise_xor((width // 2) % 2, high)
+    outer = odd * half + (1 - odd) * mixed
+    low_y = odd * high + (1 - odd) * half
+    return 32 * outer + 16 * odd + 8 * low_y + 4 * core
+
+
+def partner(c, w):
+    outer, odd, low_y, core = c // 32, (c // 16) % 2, (c // 8) % 2, (c // 4) % 2
+    if odd:
+        high = low_y
+    else:
+        high = int((w // 2) % 2 == outer)
+    other = c ^ 8 if high and not odd else c
+    return other * 8 + (w ^ (4 * high + 2 * odd + core))
+
+
+def fetch(sources, targets, sems):
+    copies = [
+        pltpu.make_async_copy(source, target, sems.at[i])
+        for i, (source, target) in enumerate(zip(sources, targets))
+    ]
+    for copy in copies:
+        copy.start()
+    for copy in copies:
+        copy.wait()
+
+
+def keep_kernel(*refs):
+    count = (len(refs) - 2) // 2
+    fetch(refs[1 : count + 1], refs[count + 1 : -1], refs[-1])
+
+
+def pack_kernel(*refs):
+    sources, out, kept, (prods, grads, taps, sems) = refs[:5], refs[5], refs[6:11], refs[11:]
+    fetch(sources, kept, sems)
+    keys, values, cotangent, queries, filters = kept
     width = lax.axis_index("width")
     prod = wide(keys[...]) * wide(values[...])
     grad = wide(cotangent[...]) * wide(queries[...])
@@ -95,11 +132,10 @@
         for half in range(2):
             rows = pl.ds(16 * block + 128 * half, 16)
             piece = jnp.concatenate([prods[rows, :], grads[rows, :], own], 1)
-            place = 8 * jnp.bitwise_xor(width, block) + 4 * half
-            out[pl.ds(place, 4)] = low(pieces_of(piece))
-
-
-def spread_kernel(arrived, first, second, back, last, twist, prod_out, grad_out, lag_out):
+            out[pl.ds(stretch(width, block, half), 4)] = low(pieces_of(piece))
+
+
+def spread_kernel(arrived, first, second, back, last, twist, prod_out, grad_out, crossing):
     pair = rows_of(wide(arrived[:, :, : 2 * LANES]))
     opened = dot(first[...], low(pair))
     turns = twist[...]
@@ -117,12 +153,13 @@
     )
     lag = dot(last[...], low(jnp.concatenate([real, imag], 0)))
     lag = lag * (1.0 / (SPAN * math.sqrt(GROUP * LENGTH)))
-    lag_out[...] = low(pieces_of(lag))
-
-
-def filter_kernel(arrived, prod, grad, first, second, back, last, twist, out):
+    crossing[:, :, :LANES] = arrived[:, :, 2 * LANES :]
+    crossing[:, :, LANES:] = low(pieces_of(lag))
+
+
+def filter_kernel(crossed, prod, grad, first, second, back, last, twist, out):
     turns = twist[...]
-    opened = dot(first[...], low(rows_of(wide(arrived[...]))))
+    opened = dot(first[...], low(rows_of(wide(crossed[:, :, :LANES]))))
     taps = spectrum(opened, turns, second[...])
     taps_real, taps_imag = taps[:, :LANES], taps[:, LANES:]
     prod_real, prod_imag = wide(prod[:, :LANES]), wide(prod[:, LANES:])
@@ -135,7 +172,8 @@
         [jnp.concatenate([real, imag], 1), jnp.concatenate([imag, -real], 1)], 0
     )
     both = dot(last[...], stacked) * (1.0 / SPAN)
-    out[...] = low(pieces_of(both))
+    out[:, :, : 2 * LANES] = low(pieces_of(both))
+    out[:, :, 2 * LANES :] = crossed[:, :, LANES:]
 
 
 def gate_kernel(
@@ -144,7 +182,7 @@
     width = lax.axis_index("width")
     for block in range(8):
         for half in range(2):
-            place = 8 * jnp.bitwise_xor(width, block) + 4 * half
+            place = stretch(width, block, half)
             piece = wide(arrived[pl.ds(place, 4), :, : 2 * LANES]).reshape(16, 2 * LANES)
             rows = pl.ds(16 * block + 128 * half, 16)
             resps[rows, :] = piece[:, :LANES]
@@ -166,50 +204,64 @@
     return jax.ShapeDtypeStruct(dims, jnp.bfloat16)
 
 
-def call(kernel, out_shape, scratch=(), flops=0, **kwargs):
+def call(kernel, out_shape, scratch=(), flops=0, room=24, **kwargs):
     return pl.pallas_call(
         kernel,
         out_shape=out_shape,
         scratch_shapes=scratch,
         cost_estimate=pl.CostEstimate(flops=flops, bytes_accessed=1 << 20, transcendentals=0),
-        compiler_params=pltpu.CompilerParams(vmem_limit_bytes=24 << 20),
+        compiler_params=pltpu.CompilerParams(vmem_limit_bytes=room << 20),
         **kwargs,
     )
 
 
 def on_device(first, second, back, last, twist, queries, keys, values, cotangent, filters):
-    pairs = [
-        (c * 8 + w, c * 8 + (w ^ (c // 8))) for c in range(CTX) for w in range(8)
-    ]
+    pairs = [(c * 8 + w, partner(c, w)) for c in range(CTX) for w in range(8)]
     channels, local = queries.shape
+    def like(array, memory):
+        return memory(array.shape, array.dtype)
+
+    anywhere = pl.BlockSpec(memory_space=pl.ANY)
+    sources = (keys, values, cotangent, queries, filters)
     packed = call(
         pack_kernel,
         shape(CTX, SUB, 3 * LANES),
         (
+            *(like(x, pltpu.VMEM) for x in sources),
             pltpu.VMEM((channels * SUB, LANES), jnp.float32),
             pltpu.VMEM((channels * SUB, LANES), jnp.float32),
             pltpu.VMEM((SUB * SUB, LANES), jnp.float32),
+            pltpu.SemaphoreType.DMA((len(sources),)),
         ),
-    )(keys, values, cotangent, queries, filters)
+        in_specs=[anywhere] * len(sources),
+        room=57,
+    )(*sources)
     arrived = lax.all_to_all(packed, "ctx", split_axis=0, concat_axis=0, tiled=True)
-    taps = lax.ppermute(arrived[:, :, 2 * LANES :], AXES, pairs)
-    prod, grad, lag = call(
+    sources = (first, second, back, last, twist, keys, values, cotangent, queries)
+    kept = call(
+        keep_kernel,
+        tuple(like(x, jax.ShapeDtypeStruct) for x in sources),
+        (pltpu.SemaphoreType.DMA((len(sources),)),),
+        flops=1_000_000_000,
+        in_specs=[anywhere] * (len(sources) + 1),
+    )(packed, *sources)
+    fixed, gates = kept[:5], kept[5:]
+    prod, grad, crossing = call(
         spread_kernel,
-        (shape(COLS, 2 * LANES), shape(COLS, 2 * LANES), shape(CTX, SUB, LANES)),
+        (shape(COLS, 2 * LANES), shape(COLS, 2 * LANES), shape(CTX, SUB, 2 * LANES)),
         flops=400_000_000,
-    )(arrived, first, second, back, last, twist)
-    lag = lax.ppermute(lag, AXES, pairs)
-    both = call(
-        filter_kernel, shape(CTX, SUB, 2 * LANES), flops=340_000_000
-    )(taps, prod, grad, first, second, back, last, twist)
-    outgoing = jnp.concatenate([both, lag], -1)
+    )(arrived, *fixed)
+    crossed = lax.ppermute(crossing, AXES, pairs)
+    outgoing = call(filter_kernel, shape(CTX, SUB, 3 * LANES), flops=340_000_000)(
+        crossed, prod, grad, *fixed
+    )
     returned = lax.all_to_all(outgoing, "ctx", split_axis=0, concat_axis=0, tiled=True)
     full = shape(channels, local)
     return call(
         gate_kernel,
         (full, full, full, full, shape(SUB, local)),
         (pltpu.VMEM((channels * SUB, LANES), jnp.float32),) * 2,
-    )(returned, keys, values, cotangent, queries)
+    )(returned, *gates)
 
 
 def solution(mesh):

time: 69.6 us -> 60.3 us (0.87)
  the two profiles are of different devices: /device:TPU:9 before, /device:TPU:16 now
where the time goes in v2:
time: 60.3 us; the launch traced here: 59.9 us
  blocking collectives  27.1 us (45%)
  starting transfers between devices  15.6 us (26%)
  waiting for transfers between devices  7.59 us (13%)
  Pallas kernels  5.62 us (9%)
  local copies, waits for them, and re-layouts  3.16 us (5%)
  between operations  0.8 us (1%)
    all_to_all x1, blocking collectives, on_device(): lax.all_to_all(outgoing, 'ctx', split_axis=0, concat_axis=0, tiled=True)  27.1 us
    all_to_all x1, starting transfers between devices, on_device(): lax.all_to_all(packed, 'ctx', split_axis=0, concat_axis=0, tiled=True)  14.9 us
    all_to_all x1, waiting for transfers between devices, on_device(): lax.all_to_all(packed, 'ctx', split_axis=0, concat_axis=0, tiled=True)  7.59 us
    unnamed x20, local copies, waits for them, and re-layouts  3.16 us
    pallas_call x1, Pallas kernels, on_device(): call(pack_kernel, shape(CTX, SUB, 3 * LANES), (*(like(x, pltpu.VMEM) for...  1.87 us
  transfers between devices with their start and end apart: 2, of which 1 were waited for; matrix products, arithmetic and copies ran while one was open for 0% of the time, Pallas kernels for 2%

profile of v2, /device:TPU:16, one launch (start us, length us, event | category | flops | bytes accessed | tf_op | source)
XLA Modules:
  0.0 59.9 jit_solution(12017932868629539265)
XLA Ops:
  0.6 0.0 copy-start.4
  0.6 0.0 copy-start.8
  0.7 0.0 copy-start.9
  0.7 1.9 %shard_map.137.refs_0_ = bf16[64,4,384]{2,1,0:T(4,128)(2,1)} custom-call(bf16[64,512]{1,0:T(8,128)(2,1)} %refs_6_.1, bf16[64,512]{1,0:T(8,128)(2,1)} %refs_7_.1, bf16[64,512]{1,0:T(8,128)(2,1)} %refs_8_.1, bf16[64,512]{1,0:T(8,128)(2,1)} %refs_9_.1, f32[4,512]{1,0:T(4,128)} %refs_4_.2), custom_call_target="tpu_custom_call" | custom-call | bytes 1048576 | tf_op jit(solution)/shard_map/pallas_call | solution.py:226
  2.5 0.0 copy-start
  2.6 0.0 copy-start.1
  2.6 0.0 copy-start.2
  2.6 0.0 copy-start.3
  2.6 14.9 %all-to-all-start = ((bf16[64,4,384]{2,1,0:T(4,128)(2,1)}), bf16[64,4,384]{2,1,0:T(4,128)(2,1)S(1)}, u32[]{:S(2)}, u32[]{:S(2)}) async-start(bf16[64,4,384]{2,1,0:T(4,128)(2,1)} %shard_map.137.refs_0_), calls=%async_computation | async-start | bytes 393216 | tf_op jit(solution)/shard_map/all_to_all | solution.py:239
  17.5 0.0 copy-done.4
  17.5 0.0 copy-done.8
  17.6 0.0 copy-done.9
  17.6 0.0 copy-done
  17.6 0.0 copy-done.1
  17.6 0.0 copy-done.2
  17.6 0.0 copy-done.3
  17.6 0.0 copy-start.5
  17.6 1.0 %copy-done.5 = f32[512,256]{1,0:T(8,128)S(1)} copy-done((f32[512,256]{1,0:T(8,128)S(1)}, f32[512,256]{1,0:T(8,128)}, u32[]{:S(2)}) %copy-start.5) | copy-done | bytes 524312
  18.7 0.0 copy-start.6
  18.7 1.0 %copy-done.6 = bf16[256,1024]{1,0:T(8,128)(2,1)S(1)} copy-done((bf16[256,1024]{1,0:T(8,128)(2,1)S(1)}, bf16[256,1024]{1,0:T(8,128)(2,1)}, u32[]{:S(2)}) %copy-start.6) | copy-done | bytes 524312
  19.7 0.0 copy-start.7
  19.7 1.0 %copy-done.7 = bf16[1024,256]{1,0:T(8,128)(2,1)S(1)} copy-done((bf16[1024,256]{1,0:T(8,128)(2,1)S(1)}, bf16[1024,256]{1,0:T(8,128)(2,1)}, u32[]{:S(2)}) %copy-start.7) | copy-done | bytes 524312
  20.7 0.9 %shard_map.138 = (bf16[1024,256]{1,0:T(8,128)(2,1)S(1)}, bf16[256,256]{1,0:T(8,128)(2,1)S(1)}, bf16[256,256]{1,0:T(8,128)(2,1)S(1)}, bf16[256,1024]{1,0:T(8,128)...) custom-call(bf16[64,4,384]{2,1,0:T(4,128)(2,1)S(1)} %copy-done, ...), custom_call_target="tpu_custom_call" | custom-call | flops 1000000000 | bytes 1048576 | tf_op jit(solution)/shard_map/pallas_call | solution.py:241
  21.7 7.6 %all-to-all-done.arrived = bf16[64,4,384]{2,1,0:T(4,128)(2,1)S(1)} async-done(((bf16[64,4,384]{2,1,0:T(4,128)(2,1)}), bf16[64,4,384]{2,1,0:T(4,128)(2,1)S(1)}, u32[]{:S(2)}, u32[]{:S(2)}) %all-to-all-start) | async-done | bytes 196640 | tf_op jit(solution)/shard_map/all_to_all | solution.py:239
  29.3 1.1 %shard_map.139 = (bf16[512,256]{1,0:T(8,128)(2,1)S(1)}, bf16[512,256]{1,0:T(8,128)(2,1)S(1)}, bf16[64,4,256]{2,1,0:T(4,128)(2,1)S(1)}) custom-call(bf16[64,4,384]{2,1,0:T(4,128)(2,1)S(1)} %all-to-all-done.arrived, bf16[1024,256]{1,0:T(8,128)(2,1)S(1)} %get-tuple-element.17.first, bf16[256,256]{1,0:T(8,128)(2,1)S(1)} %get-tuple-element.18.second, ...), custom_call_target="tpu_custom_call" | custom-call | flops 400000000 | bytes 1048576 | tf_op jit(solution)/shard_map/pallas_call | solution.py:249
  30.3 0.7 %collective-permute-start = (bf16[64,4,256]{2,1,0:T(4,128)(2,1)S(1)}, bf16[64,4,256]{2,1,0:T(4,128)(2,1)S(1)}, u32[]{:S(2)}, u32[]{:S(2)}) collective-permute-start(bf16[64,4,256]{2,1,0:T(4,128)(2,1)S(1)} %get-tuple-element.22), channel_id=1, source_target_pairs={{0,68},{1,69},{2,2},{3,3},{4,64},{5,65},{6,6},{7,7},{8,76},{9,77},... | collective-permute-start | bytes 393224 | tf_op jit(solution)/shard_map/ppermute | solution.py:254
  31.0 0.0 collective-permute-done.crossed
  31.0 0.9 %shard_map.140 = bf16[64,4,384]{2,1,0:T(4,128)(2,1)S(1)} custom-call(bf16[64,4,256]{2,1,0:T(4,128)(2,1)S(1)} %collective-permute-done.crossed, bf16[512,256]{1,0:T(8,128)(2,1)S(1)} %get-tuple-element.23.prod, bf16[512,256]{1,0:T(8,128)(2,1)S(1)} %get-tuple-element.24.grad, bf16[1024,256]{1,0:T(8,128)(2,1)S(1)} %get-tuple-element.17.first, ...), custom_call_target="tpu_custom_call" | custom-call | flops 340000000 | bytes 1048576 | tf_op jit(solution)/shard_map/pallas_call | solution.py:255
  31.9 27.1 %all_to_all.10.arrived = bf16[64,4,384]{2,1,0:T(4,128)(2,1)S(1)} all-to-all(bf16[64,4,384]{2,1,0:T(4,128)(2,1)S(1)} %shard_map.140), channel_id=1, replica_groups=mesh['ctx'=64,'width'=8] {'ctx'}, dimensions={0} | all-to-all | bytes 393216 | tf_op jit(solution)/shard_map/all_to_all | solution.py:258
  59.0 0.8 %shard_map.141 = (bf16[64,512]{1,0:T(8,128)(2,1)}, bf16[64,512]{1,0:T(8,128)(2,1)}, bf16[64,512]{1,0:T(8,128)(2,1)}, bf16[64,512]{1,0:T(8,128)(2,1)}, bf16[4,512]{1,0:T(4,128)(2,1)}) custom-call(bf16[64,4,384]{2,1,0:T(4,128)(2,1)S(1)} %all_to_all.10.arrived, bf16[64,512]{1,0:T(8,128)(2,1)S(1)} %get-tuple-element.25.keys, ...), custom_call_target="tpu_custom_call" | custom-call | bytes 1048576 | tf_op jit(solution)/shard_map/pallas_call | solution.py:260
Async XLA Ops:
  0.6 16.9 %copy-start.4 = (bf16[64,512]{1,0:T(8,128)(2,1)S(1)}, bf16[64,512]{1,0:T(8,128)(2,1)}, u32[]{:S(2)}) copy-start(bf16[64,512]{1,0:T(8,128)(2,1)} %refs_9_.1) | copy-start | bytes 196612
  0.6 16.9 %copy-start.8 = (bf16[256,256]{1,0:T(8,128)(2,1)S(1)}, bf16[256,256]{1,0:T(8,128)(2,1)}, u32[]{:S(2)}) copy-start(bf16[256,256]{1,0:T(8,128)(2,1)} %constant.12.clone.refs_3_) | copy-start | bytes 393220
  0.7 16.9 %copy-start.9 = (bf16[256,256]{1,0:T(8,128)(2,1)S(1)}, bf16[256,256]{1,0:T(8,128)(2,1)}, u32[]{:S(2)}) copy-start(bf16[256,256]{1,0:T(8,128)(2,1)} %constant.11.clone.refs_2_) | copy-start | bytes 393220
  2.5 15.0 %copy-start = (bf16[64,4,384]{2,1,0:T(4,128)(2,1)S(1)}, bf16[64,4,384]{2,1,0:T(4,128)(2,1)}, u32[]{:S(2)}) copy-start(bf16[64,4,384]{2,1,0:T(4,128)(2,1)} %shard_map.137.refs_0_) | copy-start | bytes 589828
  2.6 15.0 %copy-start.1 = (bf16[64,512]{1,0:T(8,128)(2,1)S(1)}, bf16[64,512]{1,0:T(8,128)(2,1)}, u32[]{:S(2)}) copy-start(bf16[64,512]{1,0:T(8,128)(2,1)} %refs_6_.1) | copy-start | bytes 196612
  2.6 15.0 %copy-start.2 = (bf16[64,512]{1,0:T(8,128)(2,1)S(1)}, bf16[64,512]{1,0:T(8,128)(2,1)}, u32[]{:S(2)}) copy-start(bf16[64,512]{1,0:T(8,128)(2,1)} %refs_7_.1) | copy-start | bytes 196612
  2.6 15.0 %copy-start.3 = (bf16[64,512]{1,0:T(8,128)(2,1)S(1)}, bf16[64,512]{1,0:T(8,128)(2,1)}, u32[]{:S(2)}) copy-start(bf16[64,512]{1,0:T(8,128)(2,1)} %refs_8_.1) | copy-start | bytes 196612
  2.6 26.7 %all-to-all-start = ((bf16[64,4,384]{2,1,0:T(4,128)(2,1)}), bf16[64,4,384]{2,1,0:T(4,128)(2,1)S(1)}, u32[]{:S(2)}, u32[]{:S(2)}) async-start(bf16[64,4,384]{2,1,0:T(4,128)(2,1)} %shard_map.137.refs_0_), calls=%async_computation | async-start | bytes 393216 | tf_op jit(solution)/shard_map/all_to_all | solution.py:239
  17.6 1.0 %copy-start.5 = (f32[512,256]{1,0:T(8,128)S(1)}, f32[512,256]{1,0:T(8,128)}, u32[]{:S(2)}) copy-start(f32[512,256]{1,0:T(8,128)} %constant.14.clone.refs_5_) | copy-start | bytes 1572868
  18.7 1.0 %copy-start.6 = (bf16[256,1024]{1,0:T(8,128)(2,1)S(1)}, bf16[256,1024]{1,0:T(8,128)(2,1)}, u32[]{:S(2)}) copy-start(bf16[256,1024]{1,0:T(8,128)(2,1)} %constant.13.clone.refs_4_) | copy-start | bytes 1572868
  19.7 1.0 %copy-start.7 = (bf16[1024,256]{1,0:T(8,128)(2,1)S(1)}, bf16[1024,256]{1,0:T(8,128)(2,1)}, u32[]{:S(2)}) copy-start(bf16[1024,256]{1,0:T(8,128)(2,1)} %constant.10.clone.refs_1_) | copy-start | bytes 1572868
  30.3 0.7 %collective-permute-start = (bf16[64,4,256]{2,1,0:T(4,128)(2,1)S(1)}, bf16[64,4,256]{2,1,0:T(4,128)(2,1)S(1)}, u32[]{:S(2)}, u32[]{:S(2)}) collective-permute-start(bf16[64,4,256]{2,1,0:T(4,128)(2,1)S(1)} %get-tuple-element.22), channel_id=1, source_target_pairs={{0,68},{1,69},{2,2},{3,3},{4,64},{5,65},{6,6},{7,7},{8,76},{9,77},... | collective-permute-start | bytes 393224 | tf_op jit(solution)/shard_map/ppermute | solution.py:254

commit v3 on v2

--- a/solution.py
+++ b/solution.py
@@ -85,17 +85,14 @@
     odd, high, core = (turn_by // 2) % 2, turn_by // 4, turn_by % 2
     mixed = 1 - jnp.bitwise_xor((width // 2) % 2, high)
     outer = odd * half + (1 - odd) * mixed
-    low_y = odd * high + (1 - odd) * half
-    return 32 * outer + 16 * odd + 8 * low_y + 4 * core
+    low_y = odd * mixed + (1 - odd) * half
+    return 32 * outer + 16 * core + 8 * low_y + 4 * (1 - odd)
 
 
 def partner(c, w):
-    outer, odd, low_y, core = c // 32, (c // 16) % 2, (c // 8) % 2, (c // 4) % 2
-    if odd:
-        high = low_y
-    else:
-        high = int((w // 2) % 2 == outer)
-    other = c ^ 8 if high and not odd else c
+    outer, core, low_y, odd = c // 32, (c // 16) % 2, (c // 8) % 2, 1 - (c // 4) % 2
+    high = int((w // 2) % 2 == (low_y if odd else outer))
+    other = c ^ 8 if high or odd else c
     return other * 8 + (w ^ (4 * high + 2 * odd + core))
 
 

time: 60.3 us -> 59.3 us (0.983)
  blocking collectives: 27.1 us -> 20 us
  waiting for transfers between devices: 7.59 us -> 12.2 us
  starting transfers between devices: 15.6 us -> 17.2 us
    all_to_all x1, blocking collectives: 27.1 us -> 20 us  [on_device(): lax.all_to_all(outgoing, 'ctx', split_axis=0, concat_axis=0, tiled=True)]
    ppermute x1, waiting for transfers between devices: 0.01 us -> 4.63 us  [on_device(): crossed = lax.ppermute(crossing, AXES, pairs)]
    ppermute x1, starting transfers between devices: 0.67 us -> 2.23 us  [on_device(): crossed = lax.ppermute(crossing, AXES, pairs)]
  transfers between devices with their start and end apart: 2 -> 2, of which waited for: 1 -> 2; matrix products, arithmetic and copies ran while one was open for 0% -> 0% of each run, Pallas kernels for 2% -> 2%
where the time goes in v3:
time: 59.3 us; the launch traced here: 58.9 us
  blocking collectives  20 us (34%)
  starting transfers between devices  17.2 us (29%)
  waiting for transfers between devices  12.2 us (21%)
  Pallas kernels  5.62 us (9%)
  local copies, waits for them, and re-layouts  3.16 us (5%)
  between operations  0.8 us (1%)
    all_to_all x1, blocking collectives, on_device(): lax.all_to_all(outgoing, 'ctx', split_axis=0, concat_axis=0, tiled=True)  20 us
    all_to_all x1, starting transfers between devices, on_device(): lax.all_to_all(packed, 'ctx', split_axis=0, concat_axis=0, tiled=True)  14.9 us
    all_to_all x1, waiting for transfers between devices, on_device(): lax.all_to_all(packed, 'ctx', split_axis=0, concat_axis=0, tiled=True)  7.59 us
    ppermute x1, waiting for transfers between devices, on_device(): crossed = lax.ppermute(crossing, AXES, pairs)  4.63 us
    unnamed x20, local copies, waits for them, and re-layouts  3.16 us
    ppermute x1, starting transfers between devices, on_device(): crossed = lax.ppermute(crossing, AXES, pairs)  2.23 us
    pallas_call x1, Pallas kernels, on_device(): call(pack_kernel, shape(CTX, SUB, 3 * LANES), (*(like(x, pltpu.VMEM) for...  1.87 us
  transfers between devices with their start and end apart: 2, of which 2 were waited for; matrix products, arithmetic and copies ran while one was open for 0% of the time, Pallas kernels for 2%

profile of v3, /device:TPU:16, one launch (start us, length us, event | category | flops | bytes accessed | tf_op | source)
XLA Modules:
  0.0 58.9 jit_solution(7376752872729382528)
XLA Ops:
  0.6 0.0 copy-start.4
  0.6 0.0 copy-start.8
  0.7 0.0 copy-start.9
  0.7 1.9 %shard_map.137.refs_0_ = bf16[64,4,384]{2,1,0:T(4,128)(2,1)} custom-call(bf16[64,512]{1,0:T(8,128)(2,1)} %refs_6_.1, bf16[64,512]{1,0:T(8,128)(2,1)} %refs_7_.1, bf16[64,512]{1,0:T(8,128)(2,1)} %refs_8_.1, bf16[64,512]{1,0:T(8,128)(2,1)} %refs_9_.1, f32[4,512]{1,0:T(4,128)} %refs_4_.2), custom_call_target="tpu_custom_call" | custom-call | bytes 1048576 | tf_op jit(solution)/shard_map/pallas_call | solution.py:223
  2.5 0.0 copy-start
  2.6 0.0 copy-start.1
  2.6 0.0 copy-start.2
  2.6 0.0 copy-start.3
  2.6 14.9 %all-to-all-start = ((bf16[64,4,384]{2,1,0:T(4,128)(2,1)}), bf16[64,4,384]{2,1,0:T(4,128)(2,1)S(1)}, u32[]{:S(2)}, u32[]{:S(2)}) async-start(bf16[64,4,384]{2,1,0:T(4,128)(2,1)} %shard_map.137.refs_0_), calls=%async_computation | async-start | bytes 393216 | tf_op jit(solution)/shard_map/all_to_all | solution.py:236
  17.5 0.0 copy-done.4
  17.5 0.0 copy-done.8
  17.6 0.0 copy-done.9
  17.6 0.0 copy-done
  17.6 0.0 copy-done.1
  17.6 0.0 copy-done.2
  17.6 0.0 copy-done.3
  17.6 0.0 copy-start.5
  17.6 1.0 %copy-done.5 = f32[512,256]{1,0:T(8,128)S(1)} copy-done((f32[512,256]{1,0:T(8,128)S(1)}, f32[512,256]{1,0:T(8,128)}, u32[]{:S(2)}) %copy-start.5) | copy-done | bytes 524312
  18.7 0.0 copy-start.6
  18.7 1.0 %copy-done.6 = bf16[256,1024]{1,0:T(8,128)(2,1)S(1)} copy-done((bf16[256,1024]{1,0:T(8,128)(2,1)S(1)}, bf16[256,1024]{1,0:T(8,128)(2,1)}, u32[]{:S(2)}) %copy-start.6) | copy-done | bytes 524312
  19.7 0.0 copy-start.7
  19.7 1.0 %copy-done.7 = bf16[1024,256]{1,0:T(8,128)(2,1)S(1)} copy-done((bf16[1024,256]{1,0:T(8,128)(2,1)S(1)}, bf16[1024,256]{1,0:T(8,128)(2,1)}, u32[]{:S(2)}) %copy-start.7) | copy-done | bytes 524312
  20.7 0.9 %shard_map.138 = (bf16[1024,256]{1,0:T(8,128)(2,1)S(1)}, bf16[256,256]{1,0:T(8,128)(2,1)S(1)}, bf16[256,256]{1,0:T(8,128)(2,1)S(1)}, bf16[256,1024]{1,0:T(8,128)...) custom-call(bf16[64,4,384]{2,1,0:T(4,128)(2,1)S(1)} %copy-done, ...), custom_call_target="tpu_custom_call" | custom-call | flops 1000000000 | bytes 1048576 | tf_op jit(solution)/shard_map/pallas_call | solution.py:238
  21.7 7.6 %all-to-all-done.arrived = bf16[64,4,384]{2,1,0:T(4,128)(2,1)S(1)} async-done(((bf16[64,4,384]{2,1,0:T(4,128)(2,1)}), bf16[64,4,384]{2,1,0:T(4,128)(2,1)S(1)}, u32[]{:S(2)}, u32[]{:S(2)}) %all-to-all-start) | async-done | bytes 196640 | tf_op jit(solution)/shard_map/all_to_all | solution.py:236
  29.3 1.1 %shard_map.139 = (bf16[512,256]{1,0:T(8,128)(2,1)S(1)}, bf16[512,256]{1,0:T(8,128)(2,1)S(1)}, bf16[64,4,256]{2,1,0:T(4,128)(2,1)S(1)}) custom-call(bf16[64,4,384]{2,1,0:T(4,128)(2,1)S(1)} %all-to-all-done.arrived, bf16[1024,256]{1,0:T(8,128)(2,1)S(1)} %get-tuple-element.17.first, bf16[256,256]{1,0:T(8,128)(2,1)S(1)} %get-tuple-element.18.second, ...), custom_call_target="tpu_custom_call" | custom-call | flops 400000000 | bytes 1048576 | tf_op jit(solution)/shard_map/pallas_call | solution.py:246
  30.3 2.2 %collective-permute-start = (bf16[64,4,256]{2,1,0:T(4,128)(2,1)S(1)}, bf16[64,4,256]{2,1,0:T(4,128)(2,1)S(1)}, u32[]{:S(2)}, u32[]{:S(2)}) collective-permute-start(bf16[64,4,256]{2,1,0:T(4,128)(2,1)S(1)} %get-tuple-element.22), channel_id=1, source_target_pairs={{0,70},{1,71},{2,64},{3,65},{4,66},{5,67},{6,68},{7,69},{8,78},{9,... | collective-permute-start | bytes 393224 | tf_op jit(solution)/shard_map/ppermute | solution.py:251
  32.6 4.6 %collective-permute-done.crossed = bf16[64,4,256]{2,1,0:T(4,128)(2,1)S(1)} collective-permute-done((bf16[64,4,256]{2,1,0:T(4,128)(2,1)S(1)}, bf16[64,4,256]{2,1,0:T(4,128)(2,1)S(1)}, u32[]{:S(2)}, u32[]{:S(2)}) %collective-permute-start) | collective-permute-done | bytes 131104 | tf_op jit(solution)/shard_map/ppermute | solution.py:251
  37.2 0.9 %shard_map.140 = bf16[64,4,384]{2,1,0:T(4,128)(2,1)S(1)} custom-call(bf16[64,4,256]{2,1,0:T(4,128)(2,1)S(1)} %collective-permute-done.crossed, bf16[512,256]{1,0:T(8,128)(2,1)S(1)} %get-tuple-element.23.prod, bf16[512,256]{1,0:T(8,128)(2,1)S(1)} %get-tuple-element.24.grad, bf16[1024,256]{1,0:T(8,128)(2,1)S(1)} %get-tuple-element.17.first, ...), custom_call_target="tpu_custom_call" | custom-call | flops 340000000 | bytes 1048576 | tf_op jit(solution)/shard_map/pallas_call | solution.py:252
  38.1 20.0 %all_to_all.10.arrived = bf16[64,4,384]{2,1,0:T(4,128)(2,1)S(1)} all-to-all(bf16[64,4,384]{2,1,0:T(4,128)(2,1)S(1)} %shard_map.140), channel_id=1, replica_groups=mesh['ctx'=64,'width'=8] {'ctx'}, dimensions={0} | all-to-all | bytes 393216 | tf_op jit(solution)/shard_map/all_to_all | solution.py:255
  58.1 0.8 %shard_map.141 = (bf16[64,512]{1,0:T(8,128)(2,1)}, bf16[64,512]{1,0:T(8,128)(2,1)}, bf16[64,512]{1,0:T(8,128)(2,1)}, bf16[64,512]{1,0:T(8,128)(2,1)}, bf16[4,512]{1,0:T(4,128)(2,1)}) custom-call(bf16[64,4,384]{2,1,0:T(4,128)(2,1)S(1)} %all_to_all.10.arrived, bf16[64,512]{1,0:T(8,128)(2,1)S(1)} %get-tuple-element.25.keys, ...), custom_call_target="tpu_custom_call" | custom-call | bytes 1048576 | tf_op jit(solution)/shard_map/pallas_call | solution.py:257
Async XLA Ops:
  0.6 16.9 %copy-start.4 = (bf16[64,512]{1,0:T(8,128)(2,1)S(1)}, bf16[64,512]{1,0:T(8,128)(2,1)}, u32[]{:S(2)}) copy-start(bf16[64,512]{1,0:T(8,128)(2,1)} %refs_9_.1) | copy-start | bytes 196612
  0.6 16.9 %copy-start.8 = (bf16[256,256]{1,0:T(8,128)(2,1)S(1)}, bf16[256,256]{1,0:T(8,128)(2,1)}, u32[]{:S(2)}) copy-start(bf16[256,256]{1,0:T(8,128)(2,1)} %constant.12.clone.refs_3_) | copy-start | bytes 393220
  0.7 16.9 %copy-start.9 = (bf16[256,256]{1,0:T(8,128)(2,1)S(1)}, bf16[256,256]{1,0:T(8,128)(2,1)}, u32[]{:S(2)}) copy-start(bf16[256,256]{1,0:T(8,128)(2,1)} %constant.11.clone.refs_2_) | copy-start | bytes 393220
  2.5 15.0 %copy-start = (bf16[64,4,384]{2,1,0:T(4,128)(2,1)S(1)}, bf16[64,4,384]{2,1,0:T(4,128)(2,1)}, u32[]{:S(2)}) copy-start(bf16[64,4,384]{2,1,0:T(4,128)(2,1)} %shard_map.137.refs_0_) | copy-start | bytes 589828
  2.6 15.0 %copy-start.1 = (bf16[64,512]{1,0:T(8,128)(2,1)S(1)}, bf16[64,512]{1,0:T(8,128)(2,1)}, u32[]{:S(2)}) copy-start(bf16[64,512]{1,0:T(8,128)(2,1)} %refs_6_.1) | copy-start | bytes 196612
  2.6 15.0 %copy-start.2 = (bf16[64,512]{1,0:T(8,128)(2,1)S(1)}, bf16[64,512]{1,0:T(8,128)(2,1)}, u32[]{:S(2)}) copy-start(bf16[64,512]{1,0:T(8,128)(2,1)} %refs_7_.1) | copy-start | bytes 196612
  2.6 15.0 %copy-start.3 = (bf16[64,512]{1,0:T(8,128)(2,1)S(1)}, bf16[64,512]{1,0:T(8,128)(2,1)}, u32[]{:S(2)}) copy-start(bf16[64,512]{1,0:T(8,128)(2,1)} %refs_8_.1) | copy-start | bytes 196612
  2.6 26.7 %all-to-all-start = ((bf16[64,4,384]{2,1,0:T(4,128)(2,1)}), bf16[64,4,384]{2,1,0:T(4,128)(2,1)S(1)}, u32[]{:S(2)}, u32[]{:S(2)}) async-start(bf16[64,4,384]{2,1,0:T(4,128)(2,1)} %shard_map.137.refs_0_), calls=%async_computation | async-start | bytes 393216 | tf_op jit(solution)/shard_map/all_to_all | solution.py:236
  17.6 1.0 %copy-start.5 = (f32[512,256]{1,0:T(8,128)S(1)}, f32[512,256]{1,0:T(8,128)}, u32[]{:S(2)}) copy-start(f32[512,256]{1,0:T(8,128)} %constant.14.clone.refs_5_) | copy-start | bytes 1572868
  18.7 1.0 %copy-start.6 = (bf16[256,1024]{1,0:T(8,128)(2,1)S(1)}, bf16[256,1024]{1,0:T(8,128)(2,1)}, u32[]{:S(2)}) copy-start(bf16[256,1024]{1,0:T(8,128)(2,1)} %constant.13.clone.refs_4_) | copy-start | bytes 1572868
  19.7 1.0 %copy-start.7 = (bf16[1024,256]{1,0:T(8,128)(2,1)S(1)}, bf16[1024,256]{1,0:T(8,128)(2,1)}, u32[]{:S(2)}) copy-start(bf16[1024,256]{1,0:T(8,128)(2,1)} %constant.10.clone.refs_1_) | copy-start | bytes 1572868
  30.3 6.9 %collective-permute-start = (bf16[64,4,256]{2,1,0:T(4,128)(2,1)S(1)}, bf16[64,4,256]{2,1,0:T(4,128)(2,1)S(1)}, u32[]{:S(2)}, u32[]{:S(2)}) collective-permute-start(bf16[64,4,256]{2,1,0:T(4,128)(2,1)S(1)} %get-tuple-element.22), channel_id=1, source_target_pairs={{0,70},{1,71},{2,64},{3,65},{4,66},{5,67},{6,68},{7,69},{8,78},{9,... | collective-permute-start | bytes 393224 | tf_op jit(solution)/shard_map/ppermute | solution.py:251

commit v4 on v3

--- a/solution.py
+++ b/solution.py
@@ -15,9 +15,14 @@
 LANES = 128
 COLS = 512
 ROWS = LENGTH // LANES
+HALF = COLS // 2
+EDGE = 16
+KEPT = HALF + EDGE
 CTX = 64
 SUB = 4
 AXES = ("ctx", "width")
+ORDER_IN = np.random.RandomState(3).permutation(CTX).tolist()
+ORDER_OUT = np.random.RandomState(2).permutation(CTX).tolist()
 
 
 def grid_angles(rows, cols, period):
@@ -29,15 +34,18 @@
     def low(array):
         return np.asarray(array, dtype=np.float32).astype(ml_dtypes.bfloat16)
 
-    grid = grid_angles(COLS, ROWS, COLS)
-    first = low(np.concatenate([np.cos(grid), -np.sin(grid)], 0))
-    last = low(np.concatenate([np.cos(grid.T), -np.sin(grid.T)], 1))
+    grid = grid_angles(HALF + 1, ROWS, COLS)
+    first = np.concatenate([np.cos(grid[:HALF]), np.cos(grid[HALF:]), -np.sin(grid[1:HALF])], 0)
+    weights = np.full((COLS, 1), 2.0)
+    weights[[0, HALF]] = 1.0
+    last = low((first * weights).T)
     grid = grid_angles(LANES, LANES, LANES)
     cosine, sine = np.cos(grid), np.sin(grid)
     second = low(np.block([[cosine, -sine], [sine, cosine]]))
     back = low(np.block([[cosine, sine], [-sine, cosine]]))
-    grid = grid_angles(COLS, LANES, SPAN)
+    grid = grid_angles(HALF + 1, LANES, SPAN)[np.minimum(np.arange(KEPT), HALF)]
     twist = np.concatenate([np.cos(grid), np.sin(grid)], 1).astype(np.float32)
+    first, last = low(first)[:, row_order(ORDER_IN)], last[row_order(ORDER_OUT)]
     return first, second, back, last, twist
 
 
@@ -70,23 +78,50 @@
     return real * cosine - imag * sine, imag * cosine + real * sine
 
 
-def spectrum(opened, twist, second):
-    real, imag = turn(opened[:COLS], opened[COLS:], twist, -1)
-    return dot(low(jnp.concatenate([real, imag], 1)), second)
-
-
-def unturned(real, imag, back, twist):
-    opened = dot(low(jnp.concatenate([real, imag], 1)), back)
-    return turn(opened[:, :LANES], opened[:, LANES:], twist, 1)
-
-
-def stretch(width, block, half):
-    turn_by = jnp.bitwise_xor(width, block)
-    odd, high, core = (turn_by // 2) % 2, turn_by // 4, turn_by % 2
-    mixed = 1 - jnp.bitwise_xor((width // 2) % 2, high)
-    outer = odd * half + (1 - odd) * mixed
-    low_y = odd * mixed + (1 - odd) * half
-    return 32 * outer + 16 * core + 8 * low_y + 4 * (1 - odd)
+def top_row(shape):
+    return lax.broadcasted_iota(jnp.int32, shape, 0) == 0
+
+
+def turned(opened, twist):
+    real, imag = opened[:HALF], opened[HALF:]
+    head = imag[:8]
+    edge = jnp.broadcast_to(head[:1], (EDGE, LANES))
+    head = jnp.where(top_row(head.shape), 0.0, head)
+    real = jnp.concatenate([real, edge], 0)
+    imag = jnp.concatenate([head, imag[8:], jnp.zeros_like(edge)], 0)
+    real, imag = turn(real, imag, twist, -1)
+    return low(jnp.concatenate([real, imag], 1))
+
+
+def reopened(opened, twist):
+    real, imag = turn(opened[:, :LANES], opened[:, LANES:], twist, 1)
+    head = imag[:8]
+    head = jnp.where(top_row(head.shape), real[HALF : HALF + 8], head)
+    return low(jnp.concatenate([real[:HALF], head, imag[8:HALF]], 0))
+
+
+def channel(c, w):
+    outer, core, low_y, odd = c // 32, (c // 16) % 2, (c // 8) % 2, 1 - (c // 4) % 2
+    high = int((w // 2) % 2 == (low_y if odd else outer))
+    half = outer if odd else low_y
+    return 4 * (w ^ (4 * high + 2 * odd + core)) + c % 4 + 32 * half
+
+
+def packed_slots(order):
+    words = [[0, 0] for _ in range(CTX)]
+    for slot, c in enumerate(order):
+        for w in range(8):
+            words[channel(c, w)][w // 4] |= slot << (8 * (w % 4))
+    return words
+
+
+def slot_of(words, width):
+    word = jnp.where(width < 4, jnp.int32(words[0]), jnp.int32(words[1]))
+    return jnp.bitwise_and(jnp.right_shift(word, 8 * (width % 4)), 255)
+
+
+def row_order(order):
+    return [SUB * c + s for c in order for s in range(SUB)]
 
 
 def partner(c, w):
@@ -125,50 +160,49 @@
         grads[pl.ds(s, CTX, stride=SUB), :] = grad[:, lanes]
         taps[pl.ds(s, SUB, stride=SUB), :] = filters[:, lanes]
     own = taps[...]
-    for block in range(8):
-        for half in range(2):
-            rows = pl.ds(16 * block + 128 * half, 16)
-            piece = jnp.concatenate([prods[rows, :], grads[rows, :], own], 1)
-            out[pl.ds(stretch(width, block, half), 4)] = low(pieces_of(piece))
-
-
-def spread_kernel(arrived, first, second, back, last, twist, prod_out, grad_out, crossing):
+    words = packed_slots(ORDER_IN)
+    for first in range(0, CTX, SUB):
+        rows = pl.ds(SUB * first, SUB * SUB)
+        pieces = jnp.concatenate([prods[rows, :], grads[rows, :], own], 1)
+        pieces = low(pieces_of(pieces))
+        for i in range(SUB):
+            out[pl.ds(slot_of(words[first + i], width), 1)] = pieces[i : i + 1]
+
+
+def spread_kernel(arrived, first, second, back, last, twist, spectra, crossing):
     pair = rows_of(wide(arrived[:, :, : 2 * LANES]))
     opened = dot(first[...], low(pair))
     turns = twist[...]
-    prod = spectrum(opened[:, :LANES], turns, second[...])
-    grad = spectrum(opened[:, LANES:], turns, second[...])
-    prod_out[...] = low(prod)
-    grad_out[...] = low(grad)
-    prod_real, prod_imag = prod[:, :LANES], prod[:, LANES:]
-    grad_real, grad_imag = grad[:, :LANES], grad[:, LANES:]
-    real, imag = unturned(
-        grad_real * prod_real + grad_imag * prod_imag,
-        grad_imag * prod_real - grad_real * prod_imag,
-        back[...],
-        turns,
-    )
-    lag = dot(last[...], low(jnp.concatenate([real, imag], 0)))
+    both = [turned(opened[:, :LANES], turns), turned(opened[:, LANES:], turns)]
+    both = dot(jnp.concatenate(both, 0), second[...])
+    spectra[...] = low(both)
+    prod_real, prod_imag = both[:KEPT, :LANES], both[:KEPT, LANES:]
+    grad_real, grad_imag = both[KEPT:, :LANES], both[KEPT:, LANES:]
+    real = grad_real * prod_real + grad_imag * prod_imag
+    imag = grad_imag * prod_real - grad_real * prod_imag
+    opened = dot(low(jnp.concatenate([real, imag], 1)), back[...])
+    lag = dot(last[...], reopened(opened, turns))
     lag = lag * (1.0 / (SPAN * math.sqrt(GROUP * LENGTH)))
     crossing[:, :, :LANES] = arrived[:, :, 2 * LANES :]
     crossing[:, :, LANES:] = low(pieces_of(lag))
 
 
-def filter_kernel(crossed, prod, grad, first, second, back, last, twist, out):
+def filter_kernel(crossed, spectra, first, second, back, last, twist, out):
     turns = twist[...]
     opened = dot(first[...], low(rows_of(wide(crossed[:, :, :LANES]))))
-    taps = spectrum(opened, turns, second[...])
+    taps = dot(turned(opened, turns), second[...])
     taps_real, taps_imag = taps[:, :LANES], taps[:, LANES:]
-    prod_real, prod_imag = wide(prod[:, :LANES]), wide(prod[:, LANES:])
-    grad_real, grad_imag = wide(grad[:, :LANES]), wide(grad[:, LANES:])
-    real = taps_real * (prod_real - grad_imag) - taps_imag * (prod_imag - grad_real)
-    imag = taps_real * (prod_imag + grad_real) + taps_imag * (prod_real + grad_imag)
-    real, imag = unturned(real, imag, back[...], turns)
-    real, imag = low(real), low(imag)
-    stacked = jnp.concatenate(
-        [jnp.concatenate([real, imag], 1), jnp.concatenate([imag, -real], 1)], 0
-    )
-    both = dot(last[...], stacked) * (1.0 / SPAN)
+    prod_real, prod_imag = wide(spectra[:KEPT, :LANES]), wide(spectra[:KEPT, LANES:])
+    grad_real, grad_imag = wide(spectra[KEPT:, :LANES]), wide(spectra[KEPT:, LANES:])
+    real = taps_real * prod_real - taps_imag * prod_imag
+    imag = taps_real * prod_imag + taps_imag * prod_real
+    response = jnp.concatenate([real, imag], 1)
+    real = taps_real * grad_real + taps_imag * grad_imag
+    imag = taps_real * grad_imag - taps_imag * grad_real
+    pulled = jnp.concatenate([real, imag], 1)
+    opened = dot(low(jnp.concatenate([response, pulled], 0)), back[...])
+    pair = [reopened(opened[:KEPT], turns), reopened(opened[KEPT:], turns)]
+    both = dot(last[...], jnp.concatenate(pair, 1)) * (1.0 / SPAN)
     out[:, :, : 2 * LANES] = low(pieces_of(both))
     out[:, :, 2 * LANES :] = crossed[:, :, LANES:]
 
@@ -177,15 +211,15 @@
     arrived, keys, values, cotangent, queries, mixed, query_grad, key_grad, value_grad, filter_grad, resps, pulls
 ):
     width = lax.axis_index("width")
-    for block in range(8):
-        for half in range(2):
-            place = stretch(width, block, half)
-            piece = wide(arrived[pl.ds(place, 4), :, : 2 * LANES]).reshape(16, 2 * LANES)
-            rows = pl.ds(16 * block + 128 * half, 16)
-            resps[rows, :] = piece[:, :LANES]
-            pulls[rows, :] = piece[:, LANES:]
-    lag = wide(arrived[:, :, 2 * LANES :]).reshape(GROUP, SUB, SUB, LANES)
-    lag = jnp.sum(lag, 0)
+    words = packed_slots(ORDER_OUT)
+    for first in range(0, CTX, SUB):
+        pieces = [arrived[pl.ds(slot_of(words[first + i], width), 1)] for i in range(SUB)]
+        pieces = wide(jnp.concatenate(pieces, 0)[:, :, : 2 * LANES]).reshape(SUB * SUB, 2 * LANES)
+        rows = pl.ds(SUB * first, SUB * SUB)
+        resps[rows, :] = pieces[:, :LANES]
+        pulls[rows, :] = pieces[:, LANES:]
+    lag = wide(arrived[:, :, 2 * LANES :])
+    lag = [sum(lag[k] for k in range(CTX) if ORDER_OUT[k] % SUB == i) for i in range(SUB)]
     for s in range(SUB):
         lanes = slice(LANES * s, LANES * (s + 1))
         response = resps[pl.ds(s, CTX, stride=SUB), :]
@@ -194,7 +228,7 @@
         query_grad[:, lanes] = low(wide(cotangent[:, lanes]) * response)
         key_grad[:, lanes] = low(pulled * wide(values[:, lanes]))
         value_grad[:, lanes] = low(pulled * wide(keys[:, lanes]))
-        filter_grad[:, lanes] = low(lag[:, s, :])
+        filter_grad[:, lanes] = low(jnp.concatenate([part[s : s + 1] for part in lag], 0))
 
 
 def shape(*dims):
@@ -209,6 +243,12 @@
         cost_estimate=pl.CostEstimate(flops=flops, bytes_accessed=1 << 20, transcendentals=0),
         compiler_params=pltpu.CompilerParams(vmem_limit_bytes=room << 20),
         **kwargs,
+    )
+
+
+def exchange(pieces, order):
+    return lax.all_to_all(
+        pieces, "ctx", split_axis=0, concat_axis=0, axis_index_groups=[order], tiled=True
     )
 
 
@@ -233,7 +273,7 @@
         in_specs=[anywhere] * len(sources),
         room=57,
     )(*sources)
-    arrived = lax.all_to_all(packed, "ctx", split_axis=0, concat_axis=0, tiled=True)
+    arrived = exchange(packed, ORDER_IN)
     sources = (first, second, back, last, twist, keys, values, cotangent, queries)
     kept = call(
         keep_kernel,
@@ -243,16 +283,16 @@
         in_specs=[anywhere] * (len(sources) + 1),
     )(packed, *sources)
     fixed, gates = kept[:5], kept[5:]
-    prod, grad, crossing = call(
+    spectra, crossing = call(
         spread_kernel,
-        (shape(COLS, 2 * LANES), shape(COLS, 2 * LANES), shape(CTX, SUB, 2 * LANES)),
-        flops=400_000_000,
+        (shape(2 * KEPT, 2 * LANES), shape(CTX, SUB, 2 * LANES)),
+        flops=250_000_000,
     )(arrived, *fixed)
     crossed = lax.ppermute(crossing, AXES, pairs)
-    outgoing = call(filter_kernel, shape(CTX, SUB, 3 * LANES), flops=340_000_000)(
-        crossed, prod, grad, *fixed
+    outgoing = call(filter_kernel, shape(CTX, SUB, 3 * LANES), flops=250_000_000)(
+        crossed, spectra, *fixed
     )
-    returned = lax.all_to_all(outgoing, "ctx", split_axis=0, concat_axis=0, tiled=True)
+    returned = exchange(outgoing, ORDER_OUT)
     full = shape(channels, local)
     return call(
         gate_kernel,

time: 59.3 us -> 55.5 us (0.936)
  the two profiles are of different devices: /device:TPU:16 before, /device:TPU:6 now
where the time goes in v4:
time: 55.5 us; the launch traced here: 54.7 us
  starting transfers between devices  19.8 us (36%)
  blocking collectives  18.8 us (34%)
  waiting for transfers between devices  6.31 us (11%)
  Pallas kernels  5.31 us (10%)
  local copies, waits for them, and re-layouts  3.74 us (7%)
  between operations  0.78 us (1%)
    all_to_all x1, blocking collectives, exchange(): lax.all_to_all(pieces, 'ctx', split_axis=0, concat_axis=0, axis_index_gro...  18.8 us
    all_to_all x1, starting transfers between devices, exchange(): lax.all_to_all(pieces, 'ctx', split_axis=0, concat_axis=0, axis_index_gro...  15.9 us
    ppermute x1, waiting for transfers between devices, on_device(): crossed = lax.ppermute(crossing, AXES, pairs)  4.03 us
    ppermute x1, starting transfers between devices, on_device(): crossed = lax.ppermute(crossing, AXES, pairs)  3.92 us
    unnamed x20, local copies, waits for them, and re-layouts  3.74 us
    all_to_all x1, waiting for transfers between devices, exchange(): lax.all_to_all(pieces, 'ctx', split_axis=0, concat_axis=0, axis_index_gro...  2.28 us
    pallas_call x1, Pallas kernels, on_device(): call(pack_kernel, shape(CTX, SUB, 3 * LANES), (*(like(x, pltpu.VMEM) for...  1.86 us
  transfers between devices with their start and end apart: 2, of which 2 were waited for; matrix products, arithmetic and copies ran while one was open for 0% of the time, Pallas kernels for 2%

profile of v4, /device:TPU:6, one launch (start us, length us, event | category | flops | bytes accessed | tf_op | source)
XLA Modules:
  0.0 54.7 jit_solution(7339667426246933118)
XLA Ops:
  0.6 0.0 copy-start.4
  0.6 0.0 copy-start.5
  0.7 1.9 %shard_map.137.refs_0_ = bf16[64,4,384]{2,1,0:T(4,128)(2,1)} custom-call(bf16[64,512]{1,0:T(8,128)(2,1)} %refs_6_.1, bf16[64,512]{1,0:T(8,128)(2,1)} %refs_7_.1, bf16[64,512]{1,0:T(8,128)(2,1)} %refs_8_.1, bf16[64,512]{1,0:T(8,128)(2,1)} %refs_9_.1, f32[4,512]{1,0:T(4,128)} %refs_4_.2), custom_call_target="tpu_custom_call" | custom-call | bytes 1048576 | tf_op jit(solution)/shard_map/pallas_call | solution.py:263
  2.5 0.0 copy-start
  2.5 0.0 copy-start.1
  2.5 0.0 copy-start.2
  2.6 0.0 copy-start.3
  2.6 15.9 %all-to-all-start = ((bf16[64,4,384]{2,1,0:T(4,128)(2,1)}), bf16[64,4,384]{2,1,0:T(4,128)(2,1)S(1)}, u32[]{:S(2)}, u32[]{:S(2)}) async-start(bf16[64,4,384]{2,1,0:T(4,128)(2,1)} %shard_map.137.refs_0_), calls=%async_computation | async-start | bytes 393216 | tf_op jit(solution)/shard_map/all_to_all | solution.py:250
  18.4 0.0 copy-done.4
  18.5 0.0 copy-done.5
  18.5 0.0 copy-done
  18.5 0.0 copy-done.1
  18.5 0.0 copy-done.2
  18.5 0.0 copy-done.3
  18.5 0.0 copy-start.6
  18.5 0.9 %copy-done.6 = bf16[256,512]{1,0:T(8,128)(2,1)S(1)} copy-done((bf16[256,512]{1,0:T(8,128)(2,1)S(1)}, bf16[256,512]{1,0:T(8,128)(2,1)}, u32[]{:S(2)}) %copy-start.6) | copy-done | bytes 262168
  19.5 0.0 copy-start.7
  19.5 0.9 %copy-done.7 = bf16[512,256]{1,0:T(8,128)(2,1)S(1)} copy-done((bf16[512,256]{1,0:T(8,128)(2,1)S(1)}, bf16[512,256]{1,0:T(8,128)(2,1)}, u32[]{:S(2)}) %copy-start.7) | copy-done | bytes 262168
  20.4 0.0 copy-start.8
  20.4 0.9 %copy-done.8 = bf16[256,256]{1,0:T(8,128)(2,1)S(1)} copy-done((bf16[256,256]{1,0:T(8,128)(2,1)S(1)}, bf16[256,256]{1,0:T(8,128)(2,1)}, u32[]{:S(2)}) %copy-start.8) | copy-done | bytes 131096
  21.3 0.0 copy-start.9
  21.3 0.9 %copy-done.9 = bf16[256,256]{1,0:T(8,128)(2,1)S(1)} copy-done((bf16[256,256]{1,0:T(8,128)(2,1)S(1)}, bf16[256,256]{1,0:T(8,128)(2,1)}, u32[]{:S(2)}) %copy-start.9) | copy-done | bytes 131096
  22.2 0.9 %shard_map.138 = (bf16[512,256]{1,0:T(8,128)(2,1)S(1)}, bf16[256,256]{1,0:T(8,128)(2,1)S(1)}, bf16[256,256]{1,0:T(8,128)(2,1)S(1)}, bf16[256,512]{1,0:T(8,128)(2...) custom-call(bf16[64,4,384]{2,1,0:T(4,128)(2,1)S(1)} %copy-done, ...), custom_call_target="tpu_custom_call" | custom-call | flops 1000000000 | bytes 1048576 | tf_op jit(solution)/shard_map/pallas_call | solution.py:278
  23.1 2.3 %all-to-all-done.arrived = bf16[64,4,384]{2,1,0:T(4,128)(2,1)S(1)} async-done(((bf16[64,4,384]{2,1,0:T(4,128)(2,1)}), bf16[64,4,384]{2,1,0:T(4,128)(2,1)S(1)}, u32[]{:S(2)}, u32[]{:S(2)}) %all-to-all-start) | async-done | bytes 196640 | tf_op jit(solution)/shard_map/all_to_all | solution.py:250
  25.4 0.8 %shard_map.139 = (bf16[544,256]{1,0:T(8,128)(2,1)S(1)}, bf16[64,4,256]{2,1,0:T(4,128)(2,1)S(1)}) custom-call(bf16[64,4,384]{2,1,0:T(4,128)(2,1)S(1)} %all-to-all-done.arrived, bf16[512,256]{1,0:T(8,128)(2,1)S(1)} %get-tuple-element.16.first, bf16[256,256]{1,0:T(8,128)(2,1)S(1)} %get-tuple-element.17.second, bf16[256,256]{1,0:T(8,128)(2,1)S(1)} %get-tuple-element.18.back, ...), custom_call_target="tpu_custom_call" | custom-call | flops 250000000 | bytes 1048576 | tf_op jit(solution)/shard_map/pallas_call | solution.py:286
  26.2 3.9 %collective-permute-start = (bf16[64,4,256]{2,1,0:T(4,128)(2,1)S(1)}, bf16[64,4,256]{2,1,0:T(4,128)(2,1)S(1)}, u32[]{:S(2)}, u32[]{:S(2)}) collective-permute-start(bf16[64,4,256]{2,1,0:T(4,128)(2,1)S(1)} %get-tuple-element.21), channel_id=1, source_target_pairs={{0,70},{1,71},{2,64},{3,65},{4,66},{5,67},{6,68},{7,69},{8,78},{9,... | collective-permute-start | bytes 393224 | tf_op jit(solution)/shard_map/ppermute | solution.py:291
  30.1 4.0 %collective-permute-done.crossed = bf16[64,4,256]{2,1,0:T(4,128)(2,1)S(1)} collective-permute-done((bf16[64,4,256]{2,1,0:T(4,128)(2,1)S(1)}, bf16[64,4,256]{2,1,0:T(4,128)(2,1)S(1)}, u32[]{:S(2)}, u32[]{:S(2)}) %collective-permute-start) | collective-permute-done | bytes 131104 | tf_op jit(solution)/shard_map/ppermute | solution.py:291
  34.2 0.9 %shard_map.140 = bf16[64,4,384]{2,1,0:T(4,128)(2,1)S(1)} custom-call(bf16[64,4,256]{2,1,0:T(4,128)(2,1)S(1)} %collective-permute-done.crossed, bf16[544,256]{1,0:T(8,128)(2,1)S(1)} %get-tuple-element.22.spectra, bf16[512,256]{1,0:T(8,128)(2,1)S(1)} %get-tuple-element.16.first, bf16[256,256]{1,0:T(8,128)(2,1)S(1)} %get-tuple-element.17.second, ...), custom_call_target="tpu_custom_call" | custom-call | flops 250000000 | bytes 1048576 | tf_op jit(solution)/shard_map/pallas_call | solution.py:292
  35.0 18.8 %all_to_all.10.arrived = bf16[64,4,384]{2,1,0:T(4,128)(2,1)S(1)} all-to-all(bf16[64,4,384]{2,1,0:T(4,128)(2,1)S(1)} %shard_map.140), channel_id=1, replica_groups={{288,0,400,472,184,416,280,224,424,256,8,240,368,216,72,80,104,480,232,..., dimensions={0} | all-to-all | bytes 393216 | tf_op jit(solution)/shard_map/all_to_all | solution.py:250
  53.9 0.9 %shard_map.141 = (bf16[64,512]{1,0:T(8,128)(2,1)}, bf16[64,512]{1,0:T(8,128)(2,1)}, bf16[64,512]{1,0:T(8,128)(2,1)}, bf16[64,512]{1,0:T(8,128)(2,1)}, bf16[4,512]{1,0:T(4,128)(2,1)}) custom-call(bf16[64,4,384]{2,1,0:T(4,128)(2,1)S(1)} %all_to_all.10.arrived, bf16[64,512]{1,0:T(8,128)(2,1)S(1)} %get-tuple-element.23.keys, ...), custom_call_target="tpu_custom_call" | custom-call | bytes 1048576 | tf_op jit(solution)/shard_map/pallas_call | solution.py:297
Async XLA Ops:
  0.6 17.8 %copy-start.4 = (bf16[64,512]{1,0:T(8,128)(2,1)S(1)}, bf16[64,512]{1,0:T(8,128)(2,1)}, u32[]{:S(2)}) copy-start(bf16[64,512]{1,0:T(8,128)(2,1)} %refs_9_.1) | copy-start | bytes 196612
  0.6 17.8 %copy-start.5 = (f32[272,256]{1,0:T(8,128)S(1)}, f32[272,256]{1,0:T(8,128)}, u32[]{:S(2)}) copy-start(f32[272,256]{1,0:T(8,128)} %constant.14.clone.refs_5_) | copy-start | bytes 835588
  2.5 15.9 %copy-start = (bf16[64,4,384]{2,1,0:T(4,128)(2,1)S(1)}, bf16[64,4,384]{2,1,0:T(4,128)(2,1)}, u32[]{:S(2)}) copy-start(bf16[64,4,384]{2,1,0:T(4,128)(2,1)} %shard_map.137.refs_0_) | copy-start | bytes 589828
  2.5 15.9 %copy-start.1 = (bf16[64,512]{1,0:T(8,128)(2,1)S(1)}, bf16[64,512]{1,0:T(8,128)(2,1)}, u32[]{:S(2)}) copy-start(bf16[64,512]{1,0:T(8,128)(2,1)} %refs_6_.1) | copy-start | bytes 196612
  2.5 15.9 %copy-start.2 = (bf16[64,512]{1,0:T(8,128)(2,1)S(1)}, bf16[64,512]{1,0:T(8,128)(2,1)}, u32[]{:S(2)}) copy-start(bf16[64,512]{1,0:T(8,128)(2,1)} %refs_7_.1) | copy-start | bytes 196612
  2.6 15.9 %copy-start.3 = (bf16[64,512]{1,0:T(8,128)(2,1)S(1)}, bf16[64,512]{1,0:T(8,128)(2,1)}, u32[]{:S(2)}) copy-start(bf16[64,512]{1,0:T(8,128)(2,1)} %refs_8_.1) | copy-start | bytes 196612
  2.6 22.8 %all-to-all-start = ((bf16[64,4,384]{2,1,0:T(4,128)(2,1)}), bf16[64,4,384]{2,1,0:T(4,128)(2,1)S(1)}, u32[]{:S(2)}, u32[]{:S(2)}) async-start(bf16[64,4,384]{2,1,0:T(4,128)(2,1)} %shard_map.137.refs_0_), calls=%async_computation | async-start | bytes 393216 | tf_op jit(solution)/shard_map/all_to_all | solution.py:250
  18.5 1.0 %copy-start.6 = (bf16[256,512]{1,0:T(8,128)(2,1)S(1)}, bf16[256,512]{1,0:T(8,128)(2,1)}, u32[]{:S(2)}) copy-start(bf16[256,512]{1,0:T(8,128)(2,1)} %constant.13.clone.refs_4_) | copy-start | bytes 786436
  19.5 0.9 %copy-start.7 = (bf16[512,256]{1,0:T(8,128)(2,1)S(1)}, bf16[512,256]{1,0:T(8,128)(2,1)}, u32[]{:S(2)}) copy-start(bf16[512,256]{1,0:T(8,128)(2,1)} %constant.10.clone.refs_1_) | copy-start | bytes 786436
  20.4 0.9 %copy-start.8 = (bf16[256,256]{1,0:T(8,128)(2,1)S(1)}, bf16[256,256]{1,0:T(8,128)(2,1)}, u32[]{:S(2)}) copy-start(bf16[256,256]{1,0:T(8,128)(2,1)} %constant.12.clone.refs_3_) | copy-start | bytes 393220
  21.3 0.9 %copy-start.9 = (bf16[256,256]{1,0:T(8,128)(2,1)S(1)}, bf16[256,256]{1,0:T(8,128)(2,1)}, u32[]{:S(2)}) copy-start(bf16[256,256]{1,0:T(8,128)(2,1)} %constant.11.clone.refs_2_) | copy-start | bytes 393220
  26.2 8.0 %collective-permute-start = (bf16[64,4,256]{2,1,0:T(4,128)(2,1)S(1)}, bf16[64,4,256]{2,1,0:T(4,128)(2,1)S(1)}, u32[]{:S(2)}, u32[]{:S(2)}) collective-permute-start(bf16[64,4,256]{2,1,0:T(4,128)(2,1)S(1)} %get-tuple-element.21), channel_id=1, source_target_pairs={{0,70},{1,71},{2,64},{3,65},{4,66},{5,67},{6,68},{7,69},{8,78},{9,... | collective-permute-start | bytes 393224 | tf_op jit(solution)/shard_map/ppermute | solution.py:291

commit v5 on v4

--- a/solution.py
+++ b/solution.py
@@ -21,8 +21,16 @@
 CTX = 64
 SUB = 4
 AXES = ("ctx", "width")
-ORDER_IN = np.random.RandomState(3).permutation(CTX).tolist()
-ORDER_OUT = np.random.RandomState(2).permutation(CTX).tolist()
+
+
+def shuffled(seed, start):
+    order = np.random.RandomState(seed).permutation(CTX).tolist()
+    at = order.index(start)
+    return order[at:] + order[:at]
+
+
+ORDER_IN = shuffled(3, 36)
+ORDER_OUT = shuffled(9, 36)
 
 
 def grid_angles(rows, cols, period):

time: 55.5 us -> 55 us (level)
  blocking collectives: 18.8 us -> 17.3 us
  starting transfers between devices: 19.8 us -> 20.7 us
    all_to_all x1, blocking collectives: 18.8 us -> 17.3 us  [exchange(): lax.all_to_all(pieces, 'ctx', split_axis=0, concat_axis=0, axis_index_gro...]
where the time goes in v5:
time: 55 us; the launch traced here: 54 us
  starting transfers between devices  20.7 us (38%)
  blocking collectives  17.3 us (31%)
  waiting for transfers between devices  6.15 us (11%)
  Pallas kernels  5.31 us (10%)
  local copies, waits for them, and re-layouts  3.74 us (7%)
  between operations  0.78 us (1%)
    all_to_all x1, blocking collectives, exchange(): lax.all_to_all(pieces, 'ctx', split_axis=0, concat_axis=0, axis_index_gro...  17.3 us
    all_to_all x1, starting transfers between devices, exchange(): lax.all_to_all(pieces, 'ctx', split_axis=0, concat_axis=0, axis_index_gro...  16.4 us
    ppermute x1, starting transfers between devices, on_device(): crossed = lax.ppermute(crossing, AXES, pairs)  4.33 us
    ppermute x1, waiting for transfers between devices, on_device(): crossed = lax.ppermute(crossing, AXES, pairs)  4.06 us
    unnamed x20, local copies, waits for them, and re-layouts  3.74 us
    all_to_all x1, waiting for transfers between devices, exchange(): lax.all_to_all(pieces, 'ctx', split_axis=0, concat_axis=0, axis_index_gro...  2.08 us
    pallas_call x1, Pallas kernels, on_device(): call(pack_kernel, shape(CTX, SUB, 3 * LANES), (*(like(x, pltpu.VMEM) for...  1.86 us
  transfers between devices with their start and end apart: 2, of which 2 were waited for; matrix products, arithmetic and copies ran while one was open for 0% of the time, Pallas kernels for 2%

profile of v5, /device:TPU:6, one launch (start us, length us, event | category | flops | bytes accessed | tf_op | source)
XLA Modules:
  0.0 54.0 jit_solution(3671100842678240370)
XLA Ops:
  0.6 0.0 copy-start.4
  0.6 0.0 copy-start.5
  0.7 1.9 %shard_map.137.refs_0_ = bf16[64,4,384]{2,1,0:T(4,128)(2,1)} custom-call(bf16[64,512]{1,0:T(8,128)(2,1)} %refs_6_.1, bf16[64,512]{1,0:T(8,128)(2,1)} %refs_7_.1, bf16[64,512]{1,0:T(8,128)(2,1)} %refs_8_.1, bf16[64,512]{1,0:T(8,128)(2,1)} %refs_9_.1, f32[4,512]{1,0:T(4,128)} %refs_4_.2), custom_call_target="tpu_custom_call" | custom-call | bytes 1048576 | tf_op jit(solution)/shard_map/pallas_call | solution.py:271
  2.5 0.0 copy-start
  2.5 0.0 copy-start.1
  2.5 0.0 copy-start.2
  2.6 0.0 copy-start.3
  2.6 16.4 %all-to-all-start = ((bf16[64,4,384]{2,1,0:T(4,128)(2,1)}), bf16[64,4,384]{2,1,0:T(4,128)(2,1)S(1)}, u32[]{:S(2)}, u32[]{:S(2)}) async-start(bf16[64,4,384]{2,1,0:T(4,128)(2,1)} %shard_map.137.refs_0_), calls=%async_computation | async-start | bytes 393216 | tf_op jit(solution)/shard_map/all_to_all | solution.py:258
  18.9 0.0 copy-done.4
  18.9 0.0 copy-done.5
  19.0 0.0 copy-done
  19.0 0.0 copy-done.1
  19.0 0.0 copy-done.2
  19.0 0.0 copy-done.3
  19.0 0.0 copy-start.6
  19.0 0.9 %copy-done.6 = bf16[256,512]{1,0:T(8,128)(2,1)S(1)} copy-done((bf16[256,512]{1,0:T(8,128)(2,1)S(1)}, bf16[256,512]{1,0:T(8,128)(2,1)}, u32[]{:S(2)}) %copy-start.6) | copy-done | bytes 262168
  20.0 0.0 copy-start.7
  20.0 0.9 %copy-done.7 = bf16[512,256]{1,0:T(8,128)(2,1)S(1)} copy-done((bf16[512,256]{1,0:T(8,128)(2,1)S(1)}, bf16[512,256]{1,0:T(8,128)(2,1)}, u32[]{:S(2)}) %copy-start.7) | copy-done | bytes 262168
  20.9 0.0 copy-start.8
  20.9 0.9 %copy-done.8 = bf16[256,256]{1,0:T(8,128)(2,1)S(1)} copy-done((bf16[256,256]{1,0:T(8,128)(2,1)S(1)}, bf16[256,256]{1,0:T(8,128)(2,1)}, u32[]{:S(2)}) %copy-start.8) | copy-done | bytes 131096
  21.8 0.0 copy-start.9
  21.8 0.9 %copy-done.9 = bf16[256,256]{1,0:T(8,128)(2,1)S(1)} copy-done((bf16[256,256]{1,0:T(8,128)(2,1)S(1)}, bf16[256,256]{1,0:T(8,128)(2,1)}, u32[]{:S(2)}) %copy-start.9) | copy-done | bytes 131096
  22.7 0.9 %shard_map.138 = (bf16[512,256]{1,0:T(8,128)(2,1)S(1)}, bf16[256,256]{1,0:T(8,128)(2,1)S(1)}, bf16[256,256]{1,0:T(8,128)(2,1)S(1)}, bf16[256,512]{1,0:T(8,128)(2...) custom-call(bf16[64,4,384]{2,1,0:T(4,128)(2,1)S(1)} %copy-done, ...), custom_call_target="tpu_custom_call" | custom-call | flops 1000000000 | bytes 1048576 | tf_op jit(solution)/shard_map/pallas_call | solution.py:286
  23.6 2.1 %all-to-all-done.arrived = bf16[64,4,384]{2,1,0:T(4,128)(2,1)S(1)} async-done(((bf16[64,4,384]{2,1,0:T(4,128)(2,1)}), bf16[64,4,384]{2,1,0:T(4,128)(2,1)S(1)}, u32[]{:S(2)}, u32[]{:S(2)}) %all-to-all-start) | async-done | bytes 196640 | tf_op jit(solution)/shard_map/all_to_all | solution.py:258
  25.7 0.8 %shard_map.139 = (bf16[544,256]{1,0:T(8,128)(2,1)S(1)}, bf16[64,4,256]{2,1,0:T(4,128)(2,1)S(1)}) custom-call(bf16[64,4,384]{2,1,0:T(4,128)(2,1)S(1)} %all-to-all-done.arrived, bf16[512,256]{1,0:T(8,128)(2,1)S(1)} %get-tuple-element.16.first, bf16[256,256]{1,0:T(8,128)(2,1)S(1)} %get-tuple-element.17.second, bf16[256,256]{1,0:T(8,128)(2,1)S(1)} %get-tuple-element.18.back, ...), custom_call_target="tpu_custom_call" | custom-call | flops 250000000 | bytes 1048576 | tf_op jit(solution)/shard_map/pallas_call | solution.py:294
  26.5 4.3 %collective-permute-start = (bf16[64,4,256]{2,1,0:T(4,128)(2,1)S(1)}, bf16[64,4,256]{2,1,0:T(4,128)(2,1)S(1)}, u32[]{:S(2)}, u32[]{:S(2)}) collective-permute-start(bf16[64,4,256]{2,1,0:T(4,128)(2,1)S(1)} %get-tuple-element.21), channel_id=1, source_target_pairs={{0,70},{1,71},{2,64},{3,65},{4,66},{5,67},{6,68},{7,69},{8,78},{9,... | collective-permute-start | bytes 393224 | tf_op jit(solution)/shard_map/ppermute | solution.py:299
  30.9 4.1 %collective-permute-done.crossed = bf16[64,4,256]{2,1,0:T(4,128)(2,1)S(1)} collective-permute-done((bf16[64,4,256]{2,1,0:T(4,128)(2,1)S(1)}, bf16[64,4,256]{2,1,0:T(4,128)(2,1)S(1)}, u32[]{:S(2)}, u32[]{:S(2)}) %collective-permute-start) | collective-permute-done | bytes 131104 | tf_op jit(solution)/shard_map/ppermute | solution.py:299
  34.9 0.9 %shard_map.140 = bf16[64,4,384]{2,1,0:T(4,128)(2,1)S(1)} custom-call(bf16[64,4,256]{2,1,0:T(4,128)(2,1)S(1)} %collective-permute-done.crossed, bf16[544,256]{1,0:T(8,128)(2,1)S(1)} %get-tuple-element.22.spectra, bf16[512,256]{1,0:T(8,128)(2,1)S(1)} %get-tuple-element.16.first, bf16[256,256]{1,0:T(8,128)(2,1)S(1)} %get-tuple-element.17.second, ...), custom_call_target="tpu_custom_call" | custom-call | flops 250000000 | bytes 1048576 | tf_op jit(solution)/shard_map/pallas_call | solution.py:300
  35.8 17.3 %all_to_all.10.arrived = bf16[64,4,384]{2,1,0:T(4,128)(2,1)S(1)} all-to-all(bf16[64,4,384]{2,1,0:T(4,128)(2,1)S(1)} %shard_map.140), channel_id=1, replica_groups={{288,48,56,304,240,248,16,312,184,296,112,256,440,200,136,40,120,376,27..., dimensions={0} | all-to-all | bytes 393216 | tf_op jit(solution)/shard_map/all_to_all | solution.py:258
  53.1 0.9 %shard_map.141 = (bf16[64,512]{1,0:T(8,128)(2,1)}, bf16[64,512]{1,0:T(8,128)(2,1)}, bf16[64,512]{1,0:T(8,128)(2,1)}, bf16[64,512]{1,0:T(8,128)(2,1)}, bf16[4,512]{1,0:T(4,128)(2,1)}) custom-call(bf16[64,4,384]{2,1,0:T(4,128)(2,1)S(1)} %all_to_all.10.arrived, bf16[64,512]{1,0:T(8,128)(2,1)S(1)} %get-tuple-element.23.keys, ...), custom_call_target="tpu_custom_call" | custom-call | bytes 1048576 | tf_op jit(solution)/shard_map/pallas_call | solution.py:305
Async XLA Ops:
  0.6 18.3 %copy-start.4 = (bf16[64,512]{1,0:T(8,128)(2,1)S(1)}, bf16[64,512]{1,0:T(8,128)(2,1)}, u32[]{:S(2)}) copy-start(bf16[64,512]{1,0:T(8,128)(2,1)} %refs_9_.1) | copy-start | bytes 196612
  0.6 18.3 %copy-start.5 = (f32[272,256]{1,0:T(8,128)S(1)}, f32[272,256]{1,0:T(8,128)}, u32[]{:S(2)}) copy-start(f32[272,256]{1,0:T(8,128)} %constant.14.clone.refs_5_) | copy-start | bytes 835588
  2.5 16.4 %copy-start = (bf16[64,4,384]{2,1,0:T(4,128)(2,1)S(1)}, bf16[64,4,384]{2,1,0:T(4,128)(2,1)}, u32[]{:S(2)}) copy-start(bf16[64,4,384]{2,1,0:T(4,128)(2,1)} %shard_map.137.refs_0_) | copy-start | bytes 589828
  2.5 16.4 %copy-start.1 = (bf16[64,512]{1,0:T(8,128)(2,1)S(1)}, bf16[64,512]{1,0:T(8,128)(2,1)}, u32[]{:S(2)}) copy-start(bf16[64,512]{1,0:T(8,128)(2,1)} %refs_6_.1) | copy-start | bytes 196612
  2.5 16.4 %copy-start.2 = (bf16[64,512]{1,0:T(8,128)(2,1)S(1)}, bf16[64,512]{1,0:T(8,128)(2,1)}, u32[]{:S(2)}) copy-start(bf16[64,512]{1,0:T(8,128)(2,1)} %refs_7_.1) | copy-start | bytes 196612
  2.6 16.4 %copy-start.3 = (bf16[64,512]{1,0:T(8,128)(2,1)S(1)}, bf16[64,512]{1,0:T(8,128)(2,1)}, u32[]{:S(2)}) copy-start(bf16[64,512]{1,0:T(8,128)(2,1)} %refs_8_.1) | copy-start | bytes 196612
  2.6 23.1 %all-to-all-start = ((bf16[64,4,384]{2,1,0:T(4,128)(2,1)}), bf16[64,4,384]{2,1,0:T(4,128)(2,1)S(1)}, u32[]{:S(2)}, u32[]{:S(2)}) async-start(bf16[64,4,384]{2,1,0:T(4,128)(2,1)} %shard_map.137.refs_0_), calls=%async_computation | async-start | bytes 393216 | tf_op jit(solution)/shard_map/all_to_all | solution.py:258
  19.0 1.0 %copy-start.6 = (bf16[256,512]{1,0:T(8,128)(2,1)S(1)}, bf16[256,512]{1,0:T(8,128)(2,1)}, u32[]{:S(2)}) copy-start(bf16[256,512]{1,0:T(8,128)(2,1)} %constant.13.clone.refs_4_) | copy-start | bytes 786436
  20.0 0.9 %copy-start.7 = (bf16[512,256]{1,0:T(8,128)(2,1)S(1)}, bf16[512,256]{1,0:T(8,128)(2,1)}, u32[]{:S(2)}) copy-start(bf16[512,256]{1,0:T(8,128)(2,1)} %constant.10.clone.refs_1_) | copy-start | bytes 786436
  20.9 0.9 %copy-start.8 = (bf16[256,256]{1,0:T(8,128)(2,1)S(1)}, bf16[256,256]{1,0:T(8,128)(2,1)}, u32[]{:S(2)}) copy-start(bf16[256,256]{1,0:T(8,128)(2,1)} %constant.12.clone.refs_3_) | copy-start | bytes 393220
  21.8 0.9 %copy-start.9 = (bf16[256,256]{1,0:T(8,128)(2,1)S(1)}, bf16[256,256]{1,0:T(8,128)(2,1)}, u32[]{:S(2)}) copy-start(bf16[256,256]{1,0:T(8,128)(2,1)} %constant.11.clone.refs_2_) | copy-start | bytes 393220
  26.5 8.4 %collective-permute-start = (bf16[64,4,256]{2,1,0:T(4,128)(2,1)S(1)}, bf16[64,4,256]{2,1,0:T(4,128)(2,1)S(1)}, u32[]{:S(2)}, u32[]{:S(2)}) collective-permute-start(bf16[64,4,256]{2,1,0:T(4,128)(2,1)S(1)} %get-tuple-element.21), channel_id=1, source_target_pairs={{0,70},{1,71},{2,64},{3,65},{4,66},{5,67},{6,68},{7,69},{8,78},{9,... | collective-permute-start | bytes 393224 | tf_op jit(solution)/shard_map/ppermute | solution.py:299

commit v6 on v5

--- a/solution.py
+++ b/solution.py
@@ -28,6 +28,17 @@
     at = order.index(start)
     return order[at:] + order[:at]
 
+
+PARTNERS = (
+    "3e402f9c86db7a15",
+    "e125f38d6a9cb704",
+    "ae943658720dfb1c",
+    "fb84365927d1cae0",
+    "ea594268731cbd0f",
+    "3f50e28c69ad7b41",
+    "bf48259736c0aed1",
+    "f125e3d9b7c8a640",
+)
 
 ORDER_IN = shuffled(3, 36)
 ORDER_OUT = shuffled(9, 36)
@@ -108,11 +119,17 @@
     return low(jnp.concatenate([real[:HALF], head, imag[8:HALF]], 0))
 
 
+def partner(c, w):
+    y, core = 2 * (w // 2) + (c // 8) % 2, w % 2
+    other = int(PARTNERS[2 * (c // 16) + (c // 4) % 2][2 * y + core], 16)
+    y, core = other // 2, other % 2
+    return (c - c % 16 + 8 * (y % 2) + c % 8) * 8 + 2 * (y // 2) + core
+
+
 def channel(c, w):
-    outer, core, low_y, odd = c // 32, (c // 16) % 2, (c // 8) % 2, 1 - (c // 4) % 2
-    high = int((w // 2) % 2 == (low_y if odd else outer))
-    half = outer if odd else low_y
-    return 4 * (w ^ (4 * high + 2 * odd + core)) + c % 4 + 32 * half
+    row = partner(c, w) % 8
+    half = sum(partner(before, w) % 8 == row for before in range(c % 4, c, 4))
+    return 4 * row + c % 4 + 32 * half
 
 
 def packed_slots(order):
@@ -130,13 +147,6 @@
 
 def row_order(order):
     return [SUB * c + s for c in order for s in range(SUB)]
-
-
-def partner(c, w):
-    outer, core, low_y, odd = c // 32, (c // 16) % 2, (c // 8) % 2, 1 - (c // 4) % 2
-    high = int((w // 2) % 2 == (low_y if odd else outer))
-    other = c ^ 8 if high or odd else c
-    return other * 8 + (w ^ (4 * high + 2 * odd + core))
 
 
 def fetch(sources, targets, sems):

time: 55 us -> 55 us (level)
  blocking collectives: 17.3 us -> 15.7 us
  starting transfers between devices: 20.7 us -> 22.3 us
    ppermute x1, starting transfers between devices: 4.33 us -> 5.9 us  [on_device(): crossed = lax.ppermute(crossing, AXES, pairs)]
    all_to_all x1, blocking collectives: 17.3 us -> 15.7 us  [exchange(): lax.all_to_all(pieces, 'ctx', split_axis=0, concat_axis=0, axis_index_gro...]
where the time goes in v6:
time: 55 us; the launch traced here: 54.4 us
  starting transfers between devices  22.3 us (41%)
  blocking collectives  15.7 us (29%)
  waiting for transfers between devices  6.6 us (12%)
  Pallas kernels  5.31 us (10%)
  local copies, waits for them, and re-layouts  3.74 us (7%)
  between operations  0.78 us (1%)
    all_to_all x1, starting transfers between devices, exchange(): lax.all_to_all(pieces, 'ctx', split_axis=0, concat_axis=0, axis_index_gro...  16.4 us
    all_to_all x1, blocking collectives, exchange(): lax.all_to_all(pieces, 'ctx', split_axis=0, concat_axis=0, axis_index_gro...  15.7 us
    ppermute x1, starting transfers between devices, on_device(): crossed = lax.ppermute(crossing, AXES, pairs)  5.9 us
    ppermute x1, waiting for transfers between devices, on_device(): crossed = lax.ppermute(crossing, AXES, pairs)  4.52 us
    unnamed x20, local copies, waits for them, and re-layouts  3.74 us
    all_to_all x1, waiting for transfers between devices, exchange(): lax.all_to_all(pieces, 'ctx', split_axis=0, concat_axis=0, axis_index_gro...  2.08 us
    pallas_call x1, Pallas kernels, on_device(): call(pack_kernel, shape(CTX, SUB, 3 * LANES), (*(like(x, pltpu.VMEM) for...  1.86 us
  transfers between devices with their start and end apart: 2, of which 2 were waited for; matrix products, arithmetic and copies ran while one was open for 0% of the time, Pallas kernels for 2%

profile of v6, /device:TPU:6, one launch (start us, length us, event | category | flops | bytes accessed | tf_op | source)
XLA Modules:
  0.0 54.4 jit_solution(6441336771161141150)
XLA Ops:
  0.6 0.0 copy-start.4
  0.6 0.0 copy-start.5
  0.7 1.9 %shard_map.137.refs_0_ = bf16[64,4,384]{2,1,0:T(4,128)(2,1)} custom-call(bf16[64,512]{1,0:T(8,128)(2,1)} %refs_6_.1, bf16[64,512]{1,0:T(8,128)(2,1)} %refs_7_.1, bf16[64,512]{1,0:T(8,128)(2,1)} %refs_8_.1, bf16[64,512]{1,0:T(8,128)(2,1)} %refs_9_.1, f32[4,512]{1,0:T(4,128)} %refs_4_.2), custom_call_target="tpu_custom_call" | custom-call | bytes 1048576 | tf_op jit(solution)/shard_map/pallas_call | solution.py:281
  2.5 0.0 copy-start
  2.5 0.0 copy-start.1
  2.5 0.0 copy-start.2
  2.6 0.0 copy-start.3
  2.6 16.4 %all-to-all-start = ((bf16[64,4,384]{2,1,0:T(4,128)(2,1)}), bf16[64,4,384]{2,1,0:T(4,128)(2,1)S(1)}, u32[]{:S(2)}, u32[]{:S(2)}) async-start(bf16[64,4,384]{2,1,0:T(4,128)(2,1)} %shard_map.137.refs_0_), calls=%async_computation | async-start | bytes 393216 | tf_op jit(solution)/shard_map/all_to_all | solution.py:268
  18.9 0.0 copy-done.4
  18.9 0.0 copy-done.5
  19.0 0.0 copy-done
  19.0 0.0 copy-done.1
  19.0 0.0 copy-done.2
  19.0 0.0 copy-done.3
  19.0 0.0 copy-start.6
  19.0 0.9 %copy-done.6 = bf16[256,512]{1,0:T(8,128)(2,1)S(1)} copy-done((bf16[256,512]{1,0:T(8,128)(2,1)S(1)}, bf16[256,512]{1,0:T(8,128)(2,1)}, u32[]{:S(2)}) %copy-start.6) | copy-done | bytes 262168
  20.0 0.0 copy-start.7
  20.0 0.9 %copy-done.7 = bf16[512,256]{1,0:T(8,128)(2,1)S(1)} copy-done((bf16[512,256]{1,0:T(8,128)(2,1)S(1)}, bf16[512,256]{1,0:T(8,128)(2,1)}, u32[]{:S(2)}) %copy-start.7) | copy-done | bytes 262168
  20.9 0.0 copy-start.8
  20.9 0.9 %copy-done.8 = bf16[256,256]{1,0:T(8,128)(2,1)S(1)} copy-done((bf16[256,256]{1,0:T(8,128)(2,1)S(1)}, bf16[256,256]{1,0:T(8,128)(2,1)}, u32[]{:S(2)}) %copy-start.8) | copy-done | bytes 131096
  21.8 0.0 copy-start.9
  21.8 0.9 %copy-done.9 = bf16[256,256]{1,0:T(8,128)(2,1)S(1)} copy-done((bf16[256,256]{1,0:T(8,128)(2,1)S(1)}, bf16[256,256]{1,0:T(8,128)(2,1)}, u32[]{:S(2)}) %copy-start.9) | copy-done | bytes 131096
  22.7 0.9 %shard_map.138 = (bf16[512,256]{1,0:T(8,128)(2,1)S(1)}, bf16[256,256]{1,0:T(8,128)(2,1)S(1)}, bf16[256,256]{1,0:T(8,128)(2,1)S(1)}, bf16[256,512]{1,0:T(8,128)(2...) custom-call(bf16[64,4,384]{2,1,0:T(4,128)(2,1)S(1)} %copy-done, ...), custom_call_target="tpu_custom_call" | custom-call | flops 1000000000 | bytes 1048576 | tf_op jit(solution)/shard_map/pallas_call | solution.py:296
  23.6 2.1 %all-to-all-done.arrived = bf16[64,4,384]{2,1,0:T(4,128)(2,1)S(1)} async-done(((bf16[64,4,384]{2,1,0:T(4,128)(2,1)}), bf16[64,4,384]{2,1,0:T(4,128)(2,1)S(1)}, u32[]{:S(2)}, u32[]{:S(2)}) %all-to-all-start) | async-done | bytes 196640 | tf_op jit(solution)/shard_map/all_to_all | solution.py:268
  25.7 0.8 %shard_map.139 = (bf16[544,256]{1,0:T(8,128)(2,1)S(1)}, bf16[64,4,256]{2,1,0:T(4,128)(2,1)S(1)}) custom-call(bf16[64,4,384]{2,1,0:T(4,128)(2,1)S(1)} %all-to-all-done.arrived, bf16[512,256]{1,0:T(8,128)(2,1)S(1)} %get-tuple-element.16.first, bf16[256,256]{1,0:T(8,128)(2,1)S(1)} %get-tuple-element.17.second, bf16[256,256]{1,0:T(8,128)(2,1)S(1)} %get-tuple-element.18.back, ...), custom_call_target="tpu_custom_call" | custom-call | flops 250000000 | bytes 1048576 | tf_op jit(solution)/shard_map/pallas_call | solution.py:304
  26.5 5.9 %collective-permute-start = (bf16[64,4,256]{2,1,0:T(4,128)(2,1)S(1)}, bf16[64,4,256]{2,1,0:T(4,128)(2,1)S(1)}, u32[]{:S(2)}, u32[]{:S(2)}) collective-permute-start(bf16[64,4,256]{2,1,0:T(4,128)(2,1)S(1)} %get-tuple-element.21), channel_id=1, source_target_pairs={{0,65},{1,70},{2,64},{3,71},{4,4},{5,66},{6,67},{7,68},{8,73},{9,7... | collective-permute-start | bytes 393224 | tf_op jit(solution)/shard_map/ppermute | solution.py:309
  32.4 4.5 %collective-permute-done.crossed = bf16[64,4,256]{2,1,0:T(4,128)(2,1)S(1)} collective-permute-done((bf16[64,4,256]{2,1,0:T(4,128)(2,1)S(1)}, bf16[64,4,256]{2,1,0:T(4,128)(2,1)S(1)}, u32[]{:S(2)}, u32[]{:S(2)}) %collective-permute-start) | collective-permute-done | bytes 131104 | tf_op jit(solution)/shard_map/ppermute | solution.py:309
  36.9 0.9 %shard_map.140 = bf16[64,4,384]{2,1,0:T(4,128)(2,1)S(1)} custom-call(bf16[64,4,256]{2,1,0:T(4,128)(2,1)S(1)} %collective-permute-done.crossed, bf16[544,256]{1,0:T(8,128)(2,1)S(1)} %get-tuple-element.22.spectra, bf16[512,256]{1,0:T(8,128)(2,1)S(1)} %get-tuple-element.16.first, bf16[256,256]{1,0:T(8,128)(2,1)S(1)} %get-tuple-element.17.second, ...), custom_call_target="tpu_custom_call" | custom-call | flops 250000000 | bytes 1048576 | tf_op jit(solution)/shard_map/pallas_call | solution.py:310
  37.8 15.7 %all_to_all.10.arrived = bf16[64,4,384]{2,1,0:T(4,128)(2,1)S(1)} all-to-all(bf16[64,4,384]{2,1,0:T(4,128)(2,1)S(1)} %shard_map.140), channel_id=1, replica_groups={{288,48,56,304,240,248,16,312,184,296,112,256,440,200,136,40,120,376,27..., dimensions={0} | all-to-all | bytes 393216 | tf_op jit(solution)/shard_map/all_to_all | solution.py:268
  53.6 0.9 %shard_map.141 = (bf16[64,512]{1,0:T(8,128)(2,1)}, bf16[64,512]{1,0:T(8,128)(2,1)}, bf16[64,512]{1,0:T(8,128)(2,1)}, bf16[64,512]{1,0:T(8,128)(2,1)}, bf16[4,512]{1,0:T(4,128)(2,1)}) custom-call(bf16[64,4,384]{2,1,0:T(4,128)(2,1)S(1)} %all_to_all.10.arrived, bf16[64,512]{1,0:T(8,128)(2,1)S(1)} %get-tuple-element.23.keys, ...), custom_call_target="tpu_custom_call" | custom-call | bytes 1048576 | tf_op jit(solution)/shard_map/pallas_call | solution.py:315
Async XLA Ops:
  0.6 18.3 %copy-start.4 = (bf16[64,512]{1,0:T(8,128)(2,1)S(1)}, bf16[64,512]{1,0:T(8,128)(2,1)}, u32[]{:S(2)}) copy-start(bf16[64,512]{1,0:T(8,128)(2,1)} %refs_9_.1) | copy-start | bytes 196612
  0.6 18.3 %copy-start.5 = (f32[272,256]{1,0:T(8,128)S(1)}, f32[272,256]{1,0:T(8,128)}, u32[]{:S(2)}) copy-start(f32[272,256]{1,0:T(8,128)} %constant.14.clone.refs_5_) | copy-start | bytes 835588
  2.5 16.4 %copy-start = (bf16[64,4,384]{2,1,0:T(4,128)(2,1)S(1)}, bf16[64,4,384]{2,1,0:T(4,128)(2,1)}, u32[]{:S(2)}) copy-start(bf16[64,4,384]{2,1,0:T(4,128)(2,1)} %shard_map.137.refs_0_) | copy-start | bytes 589828
  2.5 16.4 %copy-start.1 = (bf16[64,512]{1,0:T(8,128)(2,1)S(1)}, bf16[64,512]{1,0:T(8,128)(2,1)}, u32[]{:S(2)}) copy-start(bf16[64,512]{1,0:T(8,128)(2,1)} %refs_6_.1) | copy-start | bytes 196612
  2.5 16.4 %copy-start.2 = (bf16[64,512]{1,0:T(8,128)(2,1)S(1)}, bf16[64,512]{1,0:T(8,128)(2,1)}, u32[]{:S(2)}) copy-start(bf16[64,512]{1,0:T(8,128)(2,1)} %refs_7_.1) | copy-start | bytes 196612
  2.6 16.4 %copy-start.3 = (bf16[64,512]{1,0:T(8,128)(2,1)S(1)}, bf16[64,512]{1,0:T(8,128)(2,1)}, u32[]{:S(2)}) copy-start(bf16[64,512]{1,0:T(8,128)(2,1)} %refs_8_.1) | copy-start | bytes 196612
  2.6 23.1 %all-to-all-start = ((bf16[64,4,384]{2,1,0:T(4,128)(2,1)}), bf16[64,4,384]{2,1,0:T(4,128)(2,1)S(1)}, u32[]{:S(2)}, u32[]{:S(2)}) async-start(bf16[64,4,384]{2,1,0:T(4,128)(2,1)} %shard_map.137.refs_0_), calls=%async_computation | async-start | bytes 393216 | tf_op jit(solution)/shard_map/all_to_all | solution.py:268
  19.0 1.0 %copy-start.6 = (bf16[256,512]{1,0:T(8,128)(2,1)S(1)}, bf16[256,512]{1,0:T(8,128)(2,1)}, u32[]{:S(2)}) copy-start(bf16[256,512]{1,0:T(8,128)(2,1)} %constant.13.clone.refs_4_) | copy-start | bytes 786436
  20.0 0.9 %copy-start.7 = (bf16[512,256]{1,0:T(8,128)(2,1)S(1)}, bf16[512,256]{1,0:T(8,128)(2,1)}, u32[]{:S(2)}) copy-start(bf16[512,256]{1,0:T(8,128)(2,1)} %constant.10.clone.refs_1_) | copy-start | bytes 786436
  20.9 0.9 %copy-start.8 = (bf16[256,256]{1,0:T(8,128)(2,1)S(1)}, bf16[256,256]{1,0:T(8,128)(2,1)}, u32[]{:S(2)}) copy-start(bf16[256,256]{1,0:T(8,128)(2,1)} %constant.12.clone.refs_3_) | copy-start | bytes 393220
  21.8 0.9 %copy-start.9 = (bf16[256,256]{1,0:T(8,128)(2,1)S(1)}, bf16[256,256]{1,0:T(8,128)(2,1)}, u32[]{:S(2)}) copy-start(bf16[256,256]{1,0:T(8,128)(2,1)} %constant.11.clone.refs_2_) | copy-start | bytes 393220
  26.5 10.4 %collective-permute-start = (bf16[64,4,256]{2,1,0:T(4,128)(2,1)S(1)}, bf16[64,4,256]{2,1,0:T(4,128)(2,1)S(1)}, u32[]{:S(2)}, u32[]{:S(2)}) collective-permute-start(bf16[64,4,256]{2,1,0:T(4,128)(2,1)S(1)} %get-tuple-element.21), channel_id=1, source_target_pairs={{0,65},{1,70},{2,64},{3,71},{4,4},{5,66},{6,67},{7,68},{8,73},{9,7... | collective-permute-start | bytes 393224 | tf_op jit(solution)/shard_map/ppermute | solution.py:309

commit v7 on v6

--- a/solution.py
+++ b/solution.py
@@ -225,9 +225,10 @@
     out[:, :, 2 * LANES :] = crossed[:, :, LANES:]
 
 
-def gate_kernel(
-    arrived, keys, values, cotangent, queries, mixed, query_grad, key_grad, value_grad, filter_grad, resps, pulls
-):
+def gate_kernel(arrived, keys, values, cotangent, queries, *refs):
+    targets, held, (resps, pulls, sems) = refs[:5], refs[5:10], refs[10:]
+    mixed, query_grad, key_grad, value_grad, filter_grad = held
+    copies = [pltpu.make_async_copy(held[i], targets[i], sems.at[i]) for i in range(5)]
     width = lax.axis_index("width")
     words = packed_slots(ORDER_OUT)
     for first in range(0, CTX, SUB):
@@ -240,13 +241,18 @@
     lag = [sum(lag[k] for k in range(CTX) if ORDER_OUT[k] % SUB == i) for i in range(SUB)]
     for s in range(SUB):
         lanes = slice(LANES * s, LANES * (s + 1))
-        response = resps[pl.ds(s, CTX, stride=SUB), :]
-        pulled = pulls[pl.ds(s, CTX, stride=SUB), :]
-        mixed[:, lanes] = low(wide(queries[:, lanes]) * response)
-        query_grad[:, lanes] = low(wide(cotangent[:, lanes]) * response)
-        key_grad[:, lanes] = low(pulled * wide(values[:, lanes]))
-        value_grad[:, lanes] = low(pulled * wide(keys[:, lanes]))
         filter_grad[:, lanes] = low(jnp.concatenate([part[s : s + 1] for part in lag], 0))
+    copies[4].start()
+    for i, (sums, gates) in enumerate(((resps, (queries, cotangent)), (pulls, (values, keys)))):
+        for s in range(SUB):
+            lanes = slice(LANES * s, LANES * (s + 1))
+            part = sums[pl.ds(s, CTX, stride=SUB), :]
+            for target, gate in zip(held[2 * i : 2 * i + 2], gates):
+                target[:, lanes] = low(part * wide(gate[:, lanes]))
+        copies[2 * i].start()
+        copies[2 * i + 1].start()
+    for copy in copies:
+        copy.wait()
 
 
 def shape(*dims):
@@ -315,7 +321,13 @@
     return call(
         gate_kernel,
         (full, full, full, full, shape(SUB, local)),
-        (pltpu.VMEM((channels * SUB, LANES), jnp.float32),) * 2,
+        (
+            *(pltpu.VMEM((channels, local), jnp.bfloat16),) * 4,
+            pltpu.VMEM((SUB, local), jnp.bfloat16),
+            *(pltpu.VMEM((channels * SUB, LANES), jnp.float32),) * 2,
+            pltpu.SemaphoreType.DMA((5,)),
+        ),
+        out_specs=[anywhere] * 5,
     )(returned, *gates)
 
 

time: 55 us -> 55 us (level)
  no operation moved by 1% of the time
where the time goes in v7:
time: 55 us; the launch traced here: 54.5 us
  starting transfers between devices  22.3 us (41%)
  blocking collectives  15.7 us (29%)
  waiting for transfers between devices  6.6 us (12%)
  Pallas kernels  5.34 us (10%)
  local copies, waits for them, and re-layouts  3.74 us (7%)
  between operations  0.78 us (1%)
    all_to_all x1, starting transfers between devices, exchange(): lax.all_to_all(pieces, 'ctx', split_axis=0, concat_axis=0, axis_index_gro...  16.4 us
    all_to_all x1, blocking collectives, exchange(): lax.all_to_all(pieces, 'ctx', split_axis=0, concat_axis=0, axis_index_gro...  15.7 us
    ppermute x1, starting transfers between devices, on_device(): crossed = lax.ppermute(crossing, AXES, pairs)  5.9 us
    ppermute x1, waiting for transfers between devices, on_device(): crossed = lax.ppermute(crossing, AXES, pairs)  4.52 us
    unnamed x20, local copies, waits for them, and re-layouts  3.74 us
    all_to_all x1, waiting for transfers between devices, exchange(): lax.all_to_all(pieces, 'ctx', split_axis=0, concat_axis=0, axis_index_gro...  2.08 us
    pallas_call x1, Pallas kernels, on_device(): call(pack_kernel, shape(CTX, SUB, 3 * LANES), (*(like(x, pltpu.VMEM) for...  1.86 us
  transfers between devices with their start and end apart: 2, of which 2 were waited for; matrix products, arithmetic and copies ran while one was open for 0% of the time, Pallas kernels for 2%

profile of v7, /device:TPU:6, one launch (start us, length us, event | category | flops | bytes accessed | tf_op | source)
XLA Modules:
  0.0 54.5 jit_solution(14397680480713122573)
XLA Ops:
  0.6 0.0 copy-start.4
  0.6 0.0 copy-start.5
  0.7 1.9 %shard_map.137.refs_0_ = bf16[64,4,384]{2,1,0:T(4,128)(2,1)} custom-call(bf16[64,512]{1,0:T(8,128)(2,1)} %refs_6_.1, bf16[64,512]{1,0:T(8,128)(2,1)} %refs_7_.1, bf16[64,512]{1,0:T(8,128)(2,1)} %refs_8_.1, bf16[64,512]{1,0:T(8,128)(2,1)} %refs_9_.1, f32[4,512]{1,0:T(4,128)} %refs_4_.2), custom_call_target="tpu_custom_call" | custom-call | bytes 1048576 | tf_op jit(solution)/shard_map/pallas_call | solution.py:287
  2.5 0.0 copy-start
  2.5 0.0 copy-start.1
  2.5 0.0 copy-start.2
  2.6 0.0 copy-start.3
  2.6 16.4 %all-to-all-start = ((bf16[64,4,384]{2,1,0:T(4,128)(2,1)}), bf16[64,4,384]{2,1,0:T(4,128)(2,1)S(1)}, u32[]{:S(2)}, u32[]{:S(2)}) async-start(bf16[64,4,384]{2,1,0:T(4,128)(2,1)} %shard_map.137.refs_0_), calls=%async_computation | async-start | bytes 393216 | tf_op jit(solution)/shard_map/all_to_all | solution.py:274
  18.9 0.0 copy-done.4
  18.9 0.0 copy-done.5
  19.0 0.0 copy-done
  19.0 0.0 copy-done.1
  19.0 0.0 copy-done.2
  19.0 0.0 copy-done.3
  19.0 0.0 copy-start.6
  19.0 0.9 %copy-done.6 = bf16[256,512]{1,0:T(8,128)(2,1)S(1)} copy-done((bf16[256,512]{1,0:T(8,128)(2,1)S(1)}, bf16[256,512]{1,0:T(8,128)(2,1)}, u32[]{:S(2)}) %copy-start.6) | copy-done | bytes 262168
  20.0 0.0 copy-start.7
  20.0 0.9 %copy-done.7 = bf16[512,256]{1,0:T(8,128)(2,1)S(1)} copy-done((bf16[512,256]{1,0:T(8,128)(2,1)S(1)}, bf16[512,256]{1,0:T(8,128)(2,1)}, u32[]{:S(2)}) %copy-start.7) | copy-done | bytes 262168
  20.9 0.0 copy-start.8
  20.9 0.9 %copy-done.8 = bf16[256,256]{1,0:T(8,128)(2,1)S(1)} copy-done((bf16[256,256]{1,0:T(8,128)(2,1)S(1)}, bf16[256,256]{1,0:T(8,128)(2,1)}, u32[]{:S(2)}) %copy-start.8) | copy-done | bytes 131096
  21.8 0.0 copy-start.9
  21.8 0.9 %copy-done.9 = bf16[256,256]{1,0:T(8,128)(2,1)S(1)} copy-done((bf16[256,256]{1,0:T(8,128)(2,1)S(1)}, bf16[256,256]{1,0:T(8,128)(2,1)}, u32[]{:S(2)}) %copy-start.9) | copy-done | bytes 131096
  22.7 0.9 %shard_map.138 = (bf16[512,256]{1,0:T(8,128)(2,1)S(1)}, bf16[256,256]{1,0:T(8,128)(2,1)S(1)}, bf16[256,256]{1,0:T(8,128)(2,1)S(1)}, bf16[256,512]{1,0:T(8,128)(2...) custom-call(bf16[64,4,384]{2,1,0:T(4,128)(2,1)S(1)} %copy-done, ...), custom_call_target="tpu_custom_call" | custom-call | flops 1000000000 | bytes 1048576 | tf_op jit(solution)/shard_map/pallas_call | solution.py:302
  23.6 2.1 %all-to-all-done.arrived = bf16[64,4,384]{2,1,0:T(4,128)(2,1)S(1)} async-done(((bf16[64,4,384]{2,1,0:T(4,128)(2,1)}), bf16[64,4,384]{2,1,0:T(4,128)(2,1)S(1)}, u32[]{:S(2)}, u32[]{:S(2)}) %all-to-all-start) | async-done | bytes 196640 | tf_op jit(solution)/shard_map/all_to_all | solution.py:274
  25.7 0.8 %shard_map.139 = (bf16[544,256]{1,0:T(8,128)(2,1)S(1)}, bf16[64,4,256]{2,1,0:T(4,128)(2,1)S(1)}) custom-call(bf16[64,4,384]{2,1,0:T(4,128)(2,1)S(1)} %all-to-all-done.arrived, bf16[512,256]{1,0:T(8,128)(2,1)S(1)} %get-tuple-element.16.first, bf16[256,256]{1,0:T(8,128)(2,1)S(1)} %get-tuple-element.17.second, bf16[256,256]{1,0:T(8,128)(2,1)S(1)} %get-tuple-element.18.back, ...), custom_call_target="tpu_custom_call" | custom-call | flops 250000000 | bytes 1048576 | tf_op jit(solution)/shard_map/pallas_call | solution.py:310
  26.5 5.9 %collective-permute-start = (bf16[64,4,256]{2,1,0:T(4,128)(2,1)S(1)}, bf16[64,4,256]{2,1,0:T(4,128)(2,1)S(1)}, u32[]{:S(2)}, u32[]{:S(2)}) collective-permute-start(bf16[64,4,256]{2,1,0:T(4,128)(2,1)S(1)} %get-tuple-element.21), channel_id=1, source_target_pairs={{0,65},{1,70},{2,64},{3,71},{4,4},{5,66},{6,67},{7,68},{8,73},{9,7... | collective-permute-start | bytes 393224 | tf_op jit(solution)/shard_map/ppermute | solution.py:315
  32.4 4.5 %collective-permute-done.crossed = bf16[64,4,256]{2,1,0:T(4,128)(2,1)S(1)} collective-permute-done((bf16[64,4,256]{2,1,0:T(4,128)(2,1)S(1)}, bf16[64,4,256]{2,1,0:T(4,128)(2,1)S(1)}, u32[]{:S(2)}, u32[]{:S(2)}) %collective-permute-start) | collective-permute-done | bytes 131104 | tf_op jit(solution)/shard_map/ppermute | solution.py:315
  36.9 0.9 %shard_map.140 = bf16[64,4,384]{2,1,0:T(4,128)(2,1)S(1)} custom-call(bf16[64,4,256]{2,1,0:T(4,128)(2,1)S(1)} %collective-permute-done.crossed, bf16[544,256]{1,0:T(8,128)(2,1)S(1)} %get-tuple-element.22.spectra, bf16[512,256]{1,0:T(8,128)(2,1)S(1)} %get-tuple-element.16.first, bf16[256,256]{1,0:T(8,128)(2,1)S(1)} %get-tuple-element.17.second, ...), custom_call_target="tpu_custom_call" | custom-call | flops 250000000 | bytes 1048576 | tf_op jit(solution)/shard_map/pallas_call | solution.py:316
  37.8 15.7 %all_to_all.10.arrived = bf16[64,4,384]{2,1,0:T(4,128)(2,1)S(1)} all-to-all(bf16[64,4,384]{2,1,0:T(4,128)(2,1)S(1)} %shard_map.140), channel_id=1, replica_groups={{288,48,56,304,240,248,16,312,184,296,112,256,440,200,136,40,120,376,27..., dimensions={0} | all-to-all | bytes 393216 | tf_op jit(solution)/shard_map/all_to_all | solution.py:274
  53.6 0.9 %shard_map.141 = (bf16[64,512]{1,0:T(8,128)(2,1)}, bf16[64,512]{1,0:T(8,128)(2,1)}, bf16[64,512]{1,0:T(8,128)(2,1)}, bf16[64,512]{1,0:T(8,128)(2,1)}, bf16[4,512]{1,0:T(4,128)(2,1)}) custom-call(bf16[64,4,384]{2,1,0:T(4,128)(2,1)S(1)} %all_to_all.10.arrived, bf16[64,512]{1,0:T(8,128)(2,1)S(1)} %get-tuple-element.23.keys, ...), custom_call_target="tpu_custom_call" | custom-call | bytes 1048576 | tf_op jit(solution)/shard_map/pallas_call | solution.py:321
Async XLA Ops:
  0.6 18.3 %copy-start.4 = (bf16[64,512]{1,0:T(8,128)(2,1)S(1)}, bf16[64,512]{1,0:T(8,128)(2,1)}, u32[]{:S(2)}) copy-start(bf16[64,512]{1,0:T(8,128)(2,1)} %refs_9_.1) | copy-start | bytes 196612
  0.6 18.3 %copy-start.5 = (f32[272,256]{1,0:T(8,128)S(1)}, f32[272,256]{1,0:T(8,128)}, u32[]{:S(2)}) copy-start(f32[272,256]{1,0:T(8,128)} %constant.14.clone.refs_5_) | copy-start | bytes 835588
  2.5 16.4 %copy-start = (bf16[64,4,384]{2,1,0:T(4,128)(2,1)S(1)}, bf16[64,4,384]{2,1,0:T(4,128)(2,1)}, u32[]{:S(2)}) copy-start(bf16[64,4,384]{2,1,0:T(4,128)(2,1)} %shard_map.137.refs_0_) | copy-start | bytes 589828
  2.5 16.4 %copy-start.1 = (bf16[64,512]{1,0:T(8,128)(2,1)S(1)}, bf16[64,512]{1,0:T(8,128)(2,1)}, u32[]{:S(2)}) copy-start(bf16[64,512]{1,0:T(8,128)(2,1)} %refs_6_.1) | copy-start | bytes 196612
  2.5 16.4 %copy-start.2 = (bf16[64,512]{1,0:T(8,128)(2,1)S(1)}, bf16[64,512]{1,0:T(8,128)(2,1)}, u32[]{:S(2)}) copy-start(bf16[64,512]{1,0:T(8,128)(2,1)} %refs_7_.1) | copy-start | bytes 196612
  2.6 16.4 %copy-start.3 = (bf16[64,512]{1,0:T(8,128)(2,1)S(1)}, bf16[64,512]{1,0:T(8,128)(2,1)}, u32[]{:S(2)}) copy-start(bf16[64,512]{1,0:T(8,128)(2,1)} %refs_8_.1) | copy-start | bytes 196612
  2.6 23.1 %all-to-all-start = ((bf16[64,4,384]{2,1,0:T(4,128)(2,1)}), bf16[64,4,384]{2,1,0:T(4,128)(2,1)S(1)}, u32[]{:S(2)}, u32[]{:S(2)}) async-start(bf16[64,4,384]{2,1,0:T(4,128)(2,1)} %shard_map.137.refs_0_), calls=%async_computation | async-start | bytes 393216 | tf_op jit(solution)/shard_map/all_to_all | solution.py:274
  19.0 1.0 %copy-start.6 = (bf16[256,512]{1,0:T(8,128)(2,1)S(1)}, bf16[256,512]{1,0:T(8,128)(2,1)}, u32[]{:S(2)}) copy-start(bf16[256,512]{1,0:T(8,128)(2,1)} %constant.13.clone.refs_4_) | copy-start | bytes 786436
  20.0 0.9 %copy-start.7 = (bf16[512,256]{1,0:T(8,128)(2,1)S(1)}, bf16[512,256]{1,0:T(8,128)(2,1)}, u32[]{:S(2)}) copy-start(bf16[512,256]{1,0:T(8,128)(2,1)} %constant.10.clone.refs_1_) | copy-start | bytes 786436
  20.9 0.9 %copy-start.8 = (bf16[256,256]{1,0:T(8,128)(2,1)S(1)}, bf16[256,256]{1,0:T(8,128)(2,1)}, u32[]{:S(2)}) copy-start(bf16[256,256]{1,0:T(8,128)(2,1)} %constant.12.clone.refs_3_) | copy-start | bytes 393220
  21.8 0.9 %copy-start.9 = (bf16[256,256]{1,0:T(8,128)(2,1)S(1)}, bf16[256,256]{1,0:T(8,128)(2,1)}, u32[]{:S(2)}) copy-start(bf16[256,256]{1,0:T(8,128)(2,1)} %constant.11.clone.refs_2_) | copy-start | bytes 393220
  26.5 10.4 %collective-permute-start = (bf16[64,4,256]{2,1,0:T(4,128)(2,1)S(1)}, bf16[64,4,256]{2,1,0:T(4,128)(2,1)S(1)}, u32[]{:S(2)}, u32[]{:S(2)}) collective-permute-start(bf16[64,4,256]{2,1,0:T(4,128)(2,1)S(1)} %get-tuple-element.21), channel_id=1, source_target_pairs={{0,65},{1,70},{2,64},{3,71},{4,4},{5,66},{6,67},{7,68},{8,73},{9,7... | collective-permute-start | bytes 393224 | tf_op jit(solution)/shard_map/ppermute | solution.py:315

commit v8 on v6

--- a/solution.py
+++ b/solution.py
@@ -41,7 +41,7 @@
 )
 
 ORDER_IN = shuffled(3, 36)
-ORDER_OUT = shuffled(9, 36)
+ORDER_OUT = shuffled(26, 36)
 
 
 def grid_angles(rows, cols, period):

time: 55 us -> 54.9 us (level)
  no operation moved by 1% of the time
where the time goes in v8:
time: 54.9 us; the launch traced here: 54.6 us
  starting transfers between devices  22.3 us (41%)
  blocking collectives  15.9 us (29%)
  waiting for transfers between devices  6.6 us (12%)
  Pallas kernels  5.31 us (10%)
  local copies, waits for them, and re-layouts  3.74 us (7%)
  between operations  0.78 us (1%)
    all_to_all x1, starting transfers between devices, exchange(): lax.all_to_all(pieces, 'ctx', split_axis=0, concat_axis=0, axis_index_gro...  16.4 us
    all_to_all x1, blocking collectives, exchange(): lax.all_to_all(pieces, 'ctx', split_axis=0, concat_axis=0, axis_index_gro...  15.9 us
    ppermute x1, starting transfers between devices, on_device(): crossed = lax.ppermute(crossing, AXES, pairs)  5.9 us
    ppermute x1, waiting for transfers between devices, on_device(): crossed = lax.ppermute(crossing, AXES, pairs)  4.52 us
    unnamed x20, local copies, waits for them, and re-layouts  3.74 us
    all_to_all x1, waiting for transfers between devices, exchange(): lax.all_to_all(pieces, 'ctx', split_axis=0, concat_axis=0, axis_index_gro...  2.08 us
    pallas_call x1, Pallas kernels, on_device(): call(pack_kernel, shape(CTX, SUB, 3 * LANES), (*(like(x, pltpu.VMEM) for...  1.86 us
  transfers between devices with their start and end apart: 2, of which 2 were waited for; matrix products, arithmetic and copies ran while one was open for 0% of the time, Pallas kernels for 2%

profile of v8, /device:TPU:6, one launch (start us, length us, event | category | flops | bytes accessed | tf_op | source)
XLA Modules:
  0.0 54.6 jit_solution(8072895405970745777)
XLA Ops:
  0.6 0.0 copy-start.4
  0.6 0.0 copy-start.5
  0.7 1.9 %shard_map.137.refs_0_ = bf16[64,4,384]{2,1,0:T(4,128)(2,1)} custom-call(bf16[64,512]{1,0:T(8,128)(2,1)} %refs_6_.1, bf16[64,512]{1,0:T(8,128)(2,1)} %refs_7_.1, bf16[64,512]{1,0:T(8,128)(2,1)} %refs_8_.1, bf16[64,512]{1,0:T(8,128)(2,1)} %refs_9_.1, f32[4,512]{1,0:T(4,128)} %refs_4_.2), custom_call_target="tpu_custom_call" | custom-call | bytes 1048576 | tf_op jit(solution)/shard_map/pallas_call | solution.py:281
  2.5 0.0 copy-start
  2.5 0.0 copy-start.1
  2.5 0.0 copy-start.2
  2.6 0.0 copy-start.3
  2.6 16.4 %all-to-all-start = ((bf16[64,4,384]{2,1,0:T(4,128)(2,1)}), bf16[64,4,384]{2,1,0:T(4,128)(2,1)S(1)}, u32[]{:S(2)}, u32[]{:S(2)}) async-start(bf16[64,4,384]{2,1,0:T(4,128)(2,1)} %shard_map.137.refs_0_), calls=%async_computation | async-start | bytes 393216 | tf_op jit(solution)/shard_map/all_to_all | solution.py:268
  18.9 0.0 copy-done.4
  18.9 0.0 copy-done.5
  19.0 0.0 copy-done
  19.0 0.0 copy-done.1
  19.0 0.0 copy-done.2
  19.0 0.0 copy-done.3
  19.0 0.0 copy-start.6
  19.0 0.9 %copy-done.6 = bf16[256,512]{1,0:T(8,128)(2,1)S(1)} copy-done((bf16[256,512]{1,0:T(8,128)(2,1)S(1)}, bf16[256,512]{1,0:T(8,128)(2,1)}, u32[]{:S(2)}) %copy-start.6) | copy-done | bytes 262168
  20.0 0.0 copy-start.7
  20.0 0.9 %copy-done.7 = bf16[512,256]{1,0:T(8,128)(2,1)S(1)} copy-done((bf16[512,256]{1,0:T(8,128)(2,1)S(1)}, bf16[512,256]{1,0:T(8,128)(2,1)}, u32[]{:S(2)}) %copy-start.7) | copy-done | bytes 262168
  20.9 0.0 copy-start.8
  20.9 0.9 %copy-done.8 = bf16[256,256]{1,0:T(8,128)(2,1)S(1)} copy-done((bf16[256,256]{1,0:T(8,128)(2,1)S(1)}, bf16[256,256]{1,0:T(8,128)(2,1)}, u32[]{:S(2)}) %copy-start.8) | copy-done | bytes 131096
  21.8 0.0 copy-start.9
  21.8 0.9 %copy-done.9 = bf16[256,256]{1,0:T(8,128)(2,1)S(1)} copy-done((bf16[256,256]{1,0:T(8,128)(2,1)S(1)}, bf16[256,256]{1,0:T(8,128)(2,1)}, u32[]{:S(2)}) %copy-start.9) | copy-done | bytes 131096
  22.7 0.9 %shard_map.138 = (bf16[512,256]{1,0:T(8,128)(2,1)S(1)}, bf16[256,256]{1,0:T(8,128)(2,1)S(1)}, bf16[256,256]{1,0:T(8,128)(2,1)S(1)}, bf16[256,512]{1,0:T(8,128)(2...) custom-call(bf16[64,4,384]{2,1,0:T(4,128)(2,1)S(1)} %copy-done, ...), custom_call_target="tpu_custom_call" | custom-call | flops 1000000000 | bytes 1048576 | tf_op jit(solution)/shard_map/pallas_call | solution.py:296
  23.6 2.1 %all-to-all-done.arrived = bf16[64,4,384]{2,1,0:T(4,128)(2,1)S(1)} async-done(((bf16[64,4,384]{2,1,0:T(4,128)(2,1)}), bf16[64,4,384]{2,1,0:T(4,128)(2,1)S(1)}, u32[]{:S(2)}, u32[]{:S(2)}) %all-to-all-start) | async-done | bytes 196640 | tf_op jit(solution)/shard_map/all_to_all | solution.py:268
  25.7 0.8 %shard_map.139 = (bf16[544,256]{1,0:T(8,128)(2,1)S(1)}, bf16[64,4,256]{2,1,0:T(4,128)(2,1)S(1)}) custom-call(bf16[64,4,384]{2,1,0:T(4,128)(2,1)S(1)} %all-to-all-done.arrived, bf16[512,256]{1,0:T(8,128)(2,1)S(1)} %get-tuple-element.16.first, bf16[256,256]{1,0:T(8,128)(2,1)S(1)} %get-tuple-element.17.second, bf16[256,256]{1,0:T(8,128)(2,1)S(1)} %get-tuple-element.18.back, ...), custom_call_target="tpu_custom_call" | custom-call | flops 250000000 | bytes 1048576 | tf_op jit(solution)/shard_map/pallas_call | solution.py:304
  26.5 5.9 %collective-permute-start = (bf16[64,4,256]{2,1,0:T(4,128)(2,1)S(1)}, bf16[64,4,256]{2,1,0:T(4,128)(2,1)S(1)}, u32[]{:S(2)}, u32[]{:S(2)}) collective-permute-start(bf16[64,4,256]{2,1,0:T(4,128)(2,1)S(1)} %get-tuple-element.21), channel_id=1, source_target_pairs={{0,65},{1,70},{2,64},{3,71},{4,4},{5,66},{6,67},{7,68},{8,73},{9,7... | collective-permute-start | bytes 393224 | tf_op jit(solution)/shard_map/ppermute | solution.py:309
  32.4 4.5 %collective-permute-done.crossed = bf16[64,4,256]{2,1,0:T(4,128)(2,1)S(1)} collective-permute-done((bf16[64,4,256]{2,1,0:T(4,128)(2,1)S(1)}, bf16[64,4,256]{2,1,0:T(4,128)(2,1)S(1)}, u32[]{:S(2)}, u32[]{:S(2)}) %collective-permute-start) | collective-permute-done | bytes 131104 | tf_op jit(solution)/shard_map/ppermute | solution.py:309
  36.9 0.9 %shard_map.140 = bf16[64,4,384]{2,1,0:T(4,128)(2,1)S(1)} custom-call(bf16[64,4,256]{2,1,0:T(4,128)(2,1)S(1)} %collective-permute-done.crossed, bf16[544,256]{1,0:T(8,128)(2,1)S(1)} %get-tuple-element.22.spectra, bf16[512,256]{1,0:T(8,128)(2,1)S(1)} %get-tuple-element.16.first, bf16[256,256]{1,0:T(8,128)(2,1)S(1)} %get-tuple-element.17.second, ...), custom_call_target="tpu_custom_call" | custom-call | flops 250000000 | bytes 1048576 | tf_op jit(solution)/shard_map/pallas_call | solution.py:310
  37.8 15.9 %all_to_all.10.arrived = bf16[64,4,384]{2,1,0:T(4,128)(2,1)S(1)} all-to-all(bf16[64,4,384]{2,1,0:T(4,128)(2,1)S(1)} %shard_map.140), channel_id=1, replica_groups={{288,328,128,96,144,216,464,184,336,120,240,168,192,368,200,136,360,272..., dimensions={0} | all-to-all | bytes 393216 | tf_op jit(solution)/shard_map/all_to_all | solution.py:268
  53.7 0.9 %shard_map.141 = (bf16[64,512]{1,0:T(8,128)(2,1)}, bf16[64,512]{1,0:T(8,128)(2,1)}, bf16[64,512]{1,0:T(8,128)(2,1)}, bf16[64,512]{1,0:T(8,128)(2,1)}, bf16[4,512]{1,0:T(4,128)(2,1)}) custom-call(bf16[64,4,384]{2,1,0:T(4,128)(2,1)S(1)} %all_to_all.10.arrived, bf16[64,512]{1,0:T(8,128)(2,1)S(1)} %get-tuple-element.23.keys, ...), custom_call_target="tpu_custom_call" | custom-call | bytes 1048576 | tf_op jit(solution)/shard_map/pallas_call | solution.py:315
Async XLA Ops:
  0.6 18.3 %copy-start.4 = (bf16[64,512]{1,0:T(8,128)(2,1)S(1)}, bf16[64,512]{1,0:T(8,128)(2,1)}, u32[]{:S(2)}) copy-start(bf16[64,512]{1,0:T(8,128)(2,1)} %refs_9_.1) | copy-start | bytes 196612
  0.6 18.3 %copy-start.5 = (f32[272,256]{1,0:T(8,128)S(1)}, f32[272,256]{1,0:T(8,128)}, u32[]{:S(2)}) copy-start(f32[272,256]{1,0:T(8,128)} %constant.14.clone.refs_5_) | copy-start | bytes 835588
  2.5 16.4 %copy-start = (bf16[64,4,384]{2,1,0:T(4,128)(2,1)S(1)}, bf16[64,4,384]{2,1,0:T(4,128)(2,1)}, u32[]{:S(2)}) copy-start(bf16[64,4,384]{2,1,0:T(4,128)(2,1)} %shard_map.137.refs_0_) | copy-start | bytes 589828
  2.5 16.4 %copy-start.1 = (bf16[64,512]{1,0:T(8,128)(2,1)S(1)}, bf16[64,512]{1,0:T(8,128)(2,1)}, u32[]{:S(2)}) copy-start(bf16[64,512]{1,0:T(8,128)(2,1)} %refs_6_.1) | copy-start | bytes 196612
  2.5 16.4 %copy-start.2 = (bf16[64,512]{1,0:T(8,128)(2,1)S(1)}, bf16[64,512]{1,0:T(8,128)(2,1)}, u32[]{:S(2)}) copy-start(bf16[64,512]{1,0:T(8,128)(2,1)} %refs_7_.1) | copy-start | bytes 196612
  2.6 16.4 %copy-start.3 = (bf16[64,512]{1,0:T(8,128)(2,1)S(1)}, bf16[64,512]{1,0:T(8,128)(2,1)}, u32[]{:S(2)}) copy-start(bf16[64,512]{1,0:T(8,128)(2,1)} %refs_8_.1) | copy-start | bytes 196612
  2.6 23.1 %all-to-all-start = ((bf16[64,4,384]{2,1,0:T(4,128)(2,1)}), bf16[64,4,384]{2,1,0:T(4,128)(2,1)S(1)}, u32[]{:S(2)}, u32[]{:S(2)}) async-start(bf16[64,4,384]{2,1,0:T(4,128)(2,1)} %shard_map.137.refs_0_), calls=%async_computation | async-start | bytes 393216 | tf_op jit(solution)/shard_map/all_to_all | solution.py:268
  19.0 1.0 %copy-start.6 = (bf16[256,512]{1,0:T(8,128)(2,1)S(1)}, bf16[256,512]{1,0:T(8,128)(2,1)}, u32[]{:S(2)}) copy-start(bf16[256,512]{1,0:T(8,128)(2,1)} %constant.13.clone.refs_4_) | copy-start | bytes 786436
  20.0 0.9 %copy-start.7 = (bf16[512,256]{1,0:T(8,128)(2,1)S(1)}, bf16[512,256]{1,0:T(8,128)(2,1)}, u32[]{:S(2)}) copy-start(bf16[512,256]{1,0:T(8,128)(2,1)} %constant.10.clone.refs_1_) | copy-start | bytes 786436
  20.9 0.9 %copy-start.8 = (bf16[256,256]{1,0:T(8,128)(2,1)S(1)}, bf16[256,256]{1,0:T(8,128)(2,1)}, u32[]{:S(2)}) copy-start(bf16[256,256]{1,0:T(8,128)(2,1)} %constant.12.clone.refs_3_) | copy-start | bytes 393220
  21.8 0.9 %copy-start.9 = (bf16[256,256]{1,0:T(8,128)(2,1)S(1)}, bf16[256,256]{1,0:T(8,128)(2,1)}, u32[]{:S(2)}) copy-start(bf16[256,256]{1,0:T(8,128)(2,1)} %constant.11.clone.refs_2_) | copy-start | bytes 393220
  26.5 10.4 %collective-permute-start = (bf16[64,4,256]{2,1,0:T(4,128)(2,1)S(1)}, bf16[64,4,256]{2,1,0:T(4,128)(2,1)S(1)}, u32[]{:S(2)}, u32[]{:S(2)}) collective-permute-start(bf16[64,4,256]{2,1,0:T(4,128)(2,1)S(1)} %get-tuple-element.21), channel_id=1, source_target_pairs={{0,65},{1,70},{2,64},{3,71},{4,4},{5,66},{6,67},{7,68},{8,73},{9,7... | collective-permute-start | bytes 393224 | tf_op jit(solution)/shard_map/ppermute | solution.py:309
